TPU v7x, 256 devices: a whole 4x4x8 slice. The times are simulated.
256 devices in a mesh: dp: 4 (over z_hi, core), seq: 64 (over x, z_lo, y).
Axes of the slice: x: 4, y: 4, z: 8 (z_hi: 2, z_lo: 4; z = z_hi * 4 + z_lo), core: 2. Of those that a mesh axis runs over, the one named last changes fastest.
Arguments:
- query_space: bfloat16 [4, 64, 256, 1152], P('dp', 'seq'), may hold values from -8 to 8
- key_space: bfloat16 [4, 64, 256, 1152], P('dp', 'seq'), may hold values from -8 to 8
- value_space: bfloat16 [4, 64, 256, 1152], P('dp', 'seq'), may hold values from -6 to 6
- query_time: bfloat16 [4, 64, 256, 1152], P('dp', None, 'seq'), may hold values from -8 to 8
- key_time: bfloat16 [4, 64, 256, 1152], P('dp', None, 'seq'), may hold values from -8 to 8
- value_time: bfloat16 [4, 64, 256, 1152], P('dp', None, 'seq'), may hold values from -6 to 6
- cotangent: bfloat16 [4, 64, 256, 1152], P('dp', 'seq'), may hold values from -16 to 16
- gate_space: float32 [4, 1152], P('dp'), may hold values from 0.3 to 3
- gate_time: float32 [4, 1152], P('dp'), may hold values from 0.3 to 3
- weight_space: bfloat16 [1152, 1152], replicated, may hold values from -0.1875 to 0.1875
- weight_time: bfloat16 [1152, 1152], replicated, may hold values from -0.1875 to 0.1875
Outputs:
- gradient_query_space: bfloat16 [4, 64, 256, 1152], P('dp', 'seq')
- gradient_key_space: bfloat16 [4, 64, 256, 1152], P('dp', 'seq')
- gradient_value_space: bfloat16 [4, 64, 256, 1152], P('dp', 'seq')
- gradient_query_time: bfloat16 [4, 64, 256, 1152], P('dp', 'seq')
- gradient_key_time: bfloat16 [4, 64, 256, 1152], P('dp', 'seq')
- gradient_value_time: bfloat16 [4, 64, 256, 1152], P('dp', 'seq')
- gradient_weight_space: float32 [1152, 1152], P('seq', 'dp')
- gradient_weight_time: float32 [1152, 1152], P('seq', 'dp')
All inputs are finite; a program needn't handle non-finite values.
Results may differ from a plain program's by a relative error of at most 0.013.
Values may be sent and summed in bfloat16 or wider, within the bound.
A program may use at most 128 MiB of HBM per device.

v0:
```python
import math

import jax
import jax.numpy as jnp
from jax import lax
from jax.sharding import PartitionSpec as P

HEADS = 16
HEAD_DIM = 72


def attention_backward(queries, keyset, values, upstream):
    wide = jnp.float32
    factor = 1.0 / math.sqrt(queries.shape[-1])
    scores = jnp.einsum("blche,bmche->bchlm", queries, keyset, preferred_element_type=wide) * factor
    highest = jnp.max(scores, axis=-1, keepdims=True)
    raised = jnp.exp(scores - highest)
    shares = raised / jnp.sum(raised, axis=-1, keepdims=True)
    shares_half = shares.astype(jnp.bfloat16)
    attended = jnp.einsum(
        "bchlm,bmche->blche", shares_half, values, preferred_element_type=wide
    ).astype(jnp.bfloat16)
    share_grad = jnp.einsum("blche,bmche->bchlm", upstream, values, preferred_element_type=wide)
    centre = jnp.sum(shares * share_grad, axis=-1, keepdims=True)
    score_grad = (shares * (share_grad - centre) * factor).astype(jnp.bfloat16)
    query_grad = jnp.einsum(
        "bchlm,bmche->blche", score_grad, keyset, preferred_element_type=wide
    ).astype(jnp.bfloat16)
    key_grad = jnp.einsum(
        "bchlm,blche->bmche", score_grad, queries, preferred_element_type=wide
    ).astype(jnp.bfloat16)
    value_grad = jnp.einsum(
        "bchlm,blche->bmche", shares_half, upstream, preferred_element_type=wide
    ).astype(jnp.bfloat16)
    return (query_grad, key_grad, value_grad, attended)


def project(gated, weight):
    rows = gated.reshape(-1, gated.shape[-1])
    result = lax.dot_general(
        rows, weight, (((1,), (1,)), ((), ())), preferred_element_type=jnp.float32
    )
    return result.astype(jnp.bfloat16).reshape(gated.shape)


def heads_view(array):
    shape = array.shape
    return array.reshape(shape[0], shape[1], shape[2], HEADS, HEAD_DIM)


def frame_view(array):
    shape = array.shape
    return array.reshape(shape[0] * shape[1], shape[2], 1, HEADS, HEAD_DIM)


def pair_rows(left, right):
    return lax.dot_general(
        left, right, (((0,), (0,)), ((), ())), preferred_element_type=jnp.float32
    )


def per_device(
    query_space,
    key_space,
    value_space,
    query_time,
    key_time,
    value_time,
    cotangent,
    gate_space,
    gate_time,
    weight_space,
    weight_time,
):
    wide = jnp.float32
    width = weight_space.shape[0]
    local_shape = cotangent.shape
    gated_space = (gate_space[:, None, None, :] * cotangent.astype(wide)).astype(jnp.bfloat16)
    gated_time = (gate_time[:, None, None, :] * cotangent.astype(wide)).astype(jnp.bfloat16)
    upstream_space = project(gated_space, weight_space)
    spatial = attention_backward(
        frame_view(query_space),
        frame_view(key_space),
        frame_view(value_space),
        frame_view(upstream_space),
    )
    spatial = tuple((item.reshape(local_shape) for item in spatial))
    cell_shape = query_time.shape
    upstream_time = project(gated_time, weight_time)
    crossed = lax.all_to_all(upstream_time, "seq", split_axis=2, concat_axis=1, tiled=True)
    temporal = attention_backward(
        heads_view(query_time), heads_view(key_time), heads_view(value_time), heads_view(crossed)
    )
    flat = tuple((item.reshape(cell_shape) for item in temporal))
    query_grad_time, key_grad_time, value_grad_time, attended_time = (
        lax.all_to_all(flat[0], "seq", split_axis=1, concat_axis=2, tiled=True),
        lax.all_to_all(flat[1], "seq", split_axis=1, concat_axis=2, tiled=True),
        lax.all_to_all(flat[2], "seq", split_axis=1, concat_axis=2, tiled=True),
        lax.all_to_all(flat[3], "seq", split_axis=1, concat_axis=2, tiled=True),
    )
    attended_rows_space = spatial[3].reshape(-1, width)
    gated_rows_space = gated_space.reshape(-1, width)
    attended_rows_time = attended_time.reshape(-1, width)
    gated_rows_time = gated_time.reshape(-1, width)
    total_tokens = attended_rows_space.shape[0] * lax.axis_size("dp") * lax.axis_size("seq")
    factor = 1.0 / math.sqrt(total_tokens)
    part_space = pair_rows(attended_rows_space, gated_rows_space)
    part_time = pair_rows(attended_rows_time, gated_rows_time)
    summed = lax.psum_scatter(
        jnp.stack([part_space, part_time], axis=1) * factor, "seq", scatter_dimension=0, tiled=True
    )
    final = lax.psum_scatter(
        summed.astype(jnp.bfloat16), "dp", scatter_dimension=2, tiled=True
    ).astype(jnp.float32)
    weight_grad_space = final[:, 0, :]
    weight_grad_time = final[:, 1, :]
    return (
        spatial[0],
        spatial[1],
        spatial[2],
        query_grad_time,
        key_grad_time,
        value_grad_time,
        weight_grad_space,
        weight_grad_time,
    )


def solution(mesh):
    return jax.shard_map(
        per_device,
        mesh=mesh,
        in_specs=(
            P("dp", "seq", None, None),
            P("dp", "seq", None, None),
            P("dp", "seq", None, None),
            P("dp", None, "seq", None),
            P("dp", None, "seq", None),
            P("dp", None, "seq", None),
            P("dp", "seq", None, None),
            P("dp", None),
            P("dp", None),
            P(),
            P(),
        ),
        out_specs=(
            P("dp", "seq", None, None),
            P("dp", "seq", None, None),
            P("dp", "seq", None, None),
            P("dp", "seq", None, None),
            P("dp", "seq", None, None),
            P("dp", "seq", None, None),
            P("seq", "dp"),
            P("seq", "dp"),
        ),
        check_vma=False,
    )
```

profile of v0, /device:TPU:1, one launch (start us, length us, event | category | flops | bytes accessed | tf_op | source)
XLA Modules:
  0.0 679.0 jit_solution(13835372640556734008)
XLA Ops:
  7.2 0.9 reduce.13
  8.0 0.9 copy-done
  8.9 2.1 fusion.16
  11.1 0.9 copy.210
  12.0 0.5 broadcast.69
  12.5 4.2 reduce.16
  16.7 1.2 reshape.244
  17.9 12.7 %all-to-all-start = ((bf16[64,2,2304]{2,1,0:T(2,128)(2,1)}), bf16[64,2,2304]{2,1,0:T(2,128)(2,1)S(1)}, u32[]{:S(2)}, u32[]{:S(2)}) async-start(bf16[64,2,2304]{2,1,0:T(2,128)(2,1)} %reshape.244), calls=%async_computation | async-start | bytes 1179648 | tf_op jit(solution)/shard_map/all_to_all | solution.py:90
  30.6 2.1 copy.129
  32.8 1.9 reshape.228
  34.7 2.9 reshape.224
  37.7 3.9 reshape.223
  41.6 4.9 fusion.100
  46.5 4.1 fusion.37
  50.6 1.1 convolution_convert_fusion.1
  51.6 0.2 copy.130
  51.9 0.2 copy.131
  52.2 0.5 copy-done.11
  52.7 1.1 copy.128
  53.8 1.9 copy.169
  55.7 2.5 reshape.237
  58.2 4.7 fusion.99
  62.9 3.5 convolution_convert_fusion.4
  66.4 10.5 %all-to-all-start.4 = ((bf16[1,64,4,1152]{3,2,0,1:T(4,128)(2,1)}), bf16[1,64,4,1152]{3,2,0,1:T(4,128)(2,1)}, u32[]{:S(2)}, u32[]{:S(2)}) async-start(bf16[1,64,4,1152]{3,2,0,1:T(4,128)(2,1)} %reshape.237), calls=%async_computation.4 | async-start | bytes 1179648 | tf_op jit(solution)/shard_map/all_to_all | solution.py:99
  77.0 3.8 convolution_convert_fusion.5
  80.7 2.7 fusion.105
  83.5 0.5 reshape.245
  84.0 3.4 bitcast_reduce_fusion
  87.4 1.8 reshape.227
  89.2 2.7 fusion.58
  91.9 6.2 fusion.41
  98.1 1.9 copy.166
  100.0 2.5 reshape.234
  102.5 10.6 %all-to-all-start.1 = ((bf16[1,64,4,1152]{3,2,0,1:T(4,128)(2,1)}), bf16[1,64,4,1152]{3,2,0,1:T(4,128)(2,1)S(1)}, u32[]{:S(2)}, u32[]{:S(2)}) async-start(bf16[1,64,4,1152]{3,2,0,1:T(4,128)(2,1)} %reshape.234), calls=%async_computation.1 | async-start | bytes 1179648 | tf_op jit(solution)/shard_map/all_to_all | solution.py:96
  113.2 8.1 %fusion.44 = bf16[16,256,72]{1,2,0:T(8,128)(2,1)} fusion(bf16[256,16,72]{0,2,1:T(8,128)(2,1)} %bitcast.120, f32[16,256,256]{1,2,0:T(8,128)} %fusion.105, f32[16,256,256]{1,2,0:T(8,128)} %get-tuple-element.51, f32[16,256]{1,0:T(8,128)S(1)} %get-tuple-element.50), kind=kOutput, calls=%fused_computation.40 | convolution fusion | flops 158634240 | bytes 9584640 | tf_op jit(solution)/shard_map/bchlm,bmche->blche/dot_general | solution.py:26
  121.3 2.1 copy.157
  123.4 0.6 dynamic-slice
  124.6 4.3 convolution_bitcast_fusion.1
  128.9 6.4 fusion.38
  135.3 1.9 copy.167
  137.2 2.5 reshape.235
  139.7 2.7 fusion.36
  142.5 0.7 copy.168
  143.2 2.5 reshape.236
  145.7 1.5 reshape.233
  147.2 3.3 convolution_bitcast_fusion
  150.5 9.7 %all-to-all-start.2 = ((bf16[1,64,4,1152]{3,2,0,1:T(4,128)(2,1)}), bf16[1,64,4,1152]{3,2,0,1:T(4,128)(2,1)S(1)}, u32[]{:S(2)}, u32[]{:S(2)}) async-start(bf16[1,64,4,1152]{3,2,0,1:T(4,128)(2,1)} %reshape.235), calls=%async_computation.2 | async-start | bytes 1179648 | tf_op jit(solution)/shard_map/all_to_all | solution.py:97
  160.2 4.8 maximum_multiply_fusion
  165.0 16.0 %copy.155 = f32[1152,2,1152]{2,1,0:T(2,128)} copy(f32[1152,2,1152]{2,0,1:T(8,128)S(1)} %maximum_multiply_fusion) | data formatting | bytes 21233664 | tf_op jit(solution)/shard_map/mul | solution.py:110
  181.0 10.3 %all-to-all-start.3 = ((bf16[1,64,4,1152]{3,2,0,1:T(4,128)(2,1)}), bf16[1,64,4,1152]{3,2,0,1:T(4,128)(2,1)}, u32[]{:S(2)}, u32[]{:S(2)}) async-start(bf16[1,64,4,1152]{3,2,0,1:T(4,128)(2,1)} %reshape.236), calls=%async_computation.3 | async-start | bytes 1179648 | tf_op jit(solution)/shard_map/all_to_all | solution.py:98
  191.4 390.1 %all-reduce.2 = bf16[1152,2,1152]{2,1,0:T(2,128)(2,1)} all-reduce(f32[1152,2,1152]{2,1,0:T(2,128)} %copy.155), channel_id=2, replica_groups=mesh['dp'=4,'seq'=64] {'seq'}, use_global_device_ids=true, to_apply=%region_6.0.clone | all-reduce | flops 2654208 | bytes 15925248
  581.4 0.9 dynamic-slice_convert_fusion
  582.4 0.7 copy.170
  583.1 1.0 reshape.238
  584.1 7.2 %fusion.47 = bf16[16,256,72]{1,2,0:T(8,128)(2,1)S(1)} fusion(bf16[256,16,72]{0,2,1:T(8,128)(2,1)S(1)} %bitcast.117, f32[16,256,256]{1,2,0:T(8,128)} %fusion.105, f32[16,256,256]{1,2,0:T(8,128)} %get-tuple-element.51, f32[16,256]{1,0:T(8,128)S(1)} %get-tuple-element.50), kind=kOutput, calls=%fused_computation.41 | convolution fusion | flops 158634240 | bytes 9584640 | tf_op jit(solution)/shard_map/bchlm,blche->bmche/dot_general | solution.py:29
  591.4 1.1 copy.158
  592.4 2.3 copy.159
  594.7 70.2 %reduce-scatter.4.cloned.1.call-done = bf16[288,36]{1,0:T(8,128)(2,1)} async-done(((bf16[1152,36]{1,0:T(8,128)(2,1)}), bf16[288,36]{1,0:T(8,128)(2,1)}) %reduce-scatter.4.cloned.1.call-update) | async-done | bytes 20752
  664.8 1.0 reshape.239
  665.8 0.1 copy.171
  666.0 0.6 slice_bitcast_fusion
  666.6 0.9 all_to_all.18
  667.6 2.2 all_to_all.20
  669.8 2.2 all_to_all.22
  (39 shorter events, 0.2 us)
Async XLA Ops:
  7.2 1.8 copy-start
  16.7 16.0 %copy-start.13 = (f32[1,1152]{1,0:T(1,128)S(1)}, f32[1,1152]{1,0:T(1,128)}, u32[]{:S(2)}) copy-start(f32[1,1152]{1,0:T(1,128)} %param.18) | copy-start | bytes 13828
  16.7 16.0 %copy-start.8 = (bf16[1,64,4,1152]{3,2,1,0:T(4,128)(2,1)S(1)}, bf16[1,64,4,1152]{3,2,1,0:T(4,128)(2,1)}, u32[]{:S(2)}) copy-start(bf16[1,64,4,1152]{3,2,1,0:T(4,128)(2,1)} %param.16) | copy-start | bytes 1769476
  17.9 16.8 %copy-start.9 = (bf16[1,64,4,1152]{3,2,1,0:T(4,128)(2,1)S(1)}, bf16[1,64,4,1152]{3,2,1,0:T(4,128)(2,1)}, u32[]{:S(2)}) copy-start(bf16[1,64,4,1152]{3,2,1,0:T(4,128)(2,1)} %param.15) | copy-start | bytes 1769476
  17.9 48.5 %all-to-all-start = ((bf16[64,2,2304]{2,1,0:T(2,128)(2,1)}), bf16[64,2,2304]{2,1,0:T(2,128)(2,1)S(1)}, u32[]{:S(2)}, u32[]{:S(2)}) async-start(bf16[64,2,2304]{2,1,0:T(2,128)(2,1)} %reshape.244), calls=%async_computation | async-start | bytes 1179648 | tf_op jit(solution)/shard_map/all_to_all | solution.py:90
  34.7 11.7 %copy-start.2 = (bf16[64,4,16,72]{3,2,1,0:T(8,128)(2,1)}, bf16[64,4,16,72]{3,2,1,0:T(8,128)(2,1)S(1)}, u32[]{:S(2)}) copy-start(bf16[64,4,16,72]{3,2,1,0:T(8,128)(2,1)S(1)} %reshape.228) | copy-start | bytes 1769476
  46.5 4.1 copy-start.5
  46.5 4.1 copy-start.14
  50.6 1.3 copy-start.10
  51.6 1.1 copy-start.11
  66.4 36.1 %all-to-all-start.4 = ((bf16[1,64,4,1152]{3,2,0,1:T(4,128)(2,1)}), bf16[1,64,4,1152]{3,2,0,1:T(4,128)(2,1)}, u32[]{:S(2)}, u32[]{:S(2)}) async-start(bf16[1,64,4,1152]{3,2,0,1:T(4,128)(2,1)} %reshape.237), calls=%async_computation.4 | async-start | bytes 1179648 | tf_op jit(solution)/shard_map/all_to_all | solution.py:99
  87.4 1.8 copy-start.3
  102.5 48.0 %all-to-all-start.1 = ((bf16[1,64,4,1152]{3,2,0,1:T(4,128)(2,1)}), bf16[1,64,4,1152]{3,2,0,1:T(4,128)(2,1)S(1)}, u32[]{:S(2)}, u32[]{:S(2)}) async-start(bf16[1,64,4,1152]{3,2,0,1:T(4,128)(2,1)} %reshape.234), calls=%async_computation.1 | async-start | bytes 1179648 | tf_op jit(solution)/shard_map/all_to_all | solution.py:96
  113.1 10.2 %copy-start.15 = (u32[256]{0:T(256)S(1)}, u32[256]{0:T(256)}, u32[]{:S(2)}) copy-start(u32[256]{0:T(256)} %constant.20) | copy-start | bytes 3076
  113.1 11.5 %copy-start.6 = (bf16[1,1,256,1152]{3,2,1,0:T(8,128)(2,1)S(1)}, bf16[1,1,256,1152]{3,2,1,0:T(8,128)(2,1)}, u32[]{:S(2)}) copy-start(bf16[1,1,256,1152]{3,2,1,0:T(8,128)(2,1)} %param.17) | copy-start | bytes 1769476
  142.5 4.7 copy-start.7
  150.5 30.4 %all-to-all-start.2 = ((bf16[1,64,4,1152]{3,2,0,1:T(4,128)(2,1)}), bf16[1,64,4,1152]{3,2,0,1:T(4,128)(2,1)S(1)}, u32[]{:S(2)}, u32[]{:S(2)}) async-start(bf16[1,64,4,1152]{3,2,0,1:T(4,128)(2,1)} %reshape.235), calls=%async_computation.2 | async-start | bytes 1179648 | tf_op jit(solution)/shard_map/all_to_all | solution.py:97
  181.0 400.5 %copy-start.4 = (bf16[1,64,4,1152]{3,2,0,1:T(4,128)(2,1)}, bf16[1,64,4,1152]{3,2,0,1:T(4,128)(2,1)S(1)}, u32[]{:S(2)}) copy-start(bf16[1,64,4,1152]{3,2,0,1:T(4,128)(2,1)S(1)} %all-to-all-done.2) | copy-start | bytes 1769476
  181.0 488.8 %all-to-all-start.3 = ((bf16[1,64,4,1152]{3,2,0,1:T(4,128)(2,1)}), bf16[1,64,4,1152]{3,2,0,1:T(4,128)(2,1)}, u32[]{:S(2)}, u32[]{:S(2)}) async-start(bf16[1,64,4,1152]{3,2,0,1:T(4,128)(2,1)} %reshape.236), calls=%async_computation.3 | async-start | bytes 1179648 | tf_op jit(solution)/shard_map/all_to_all | solution.py:98
  191.3 392.8 %copy-start.12 = (bf16[1,1,256,1152]{2,3,1,0:T(8,128)(2,1)S(1)}, bf16[1,1,256,1152]{2,3,1,0:T(8,128)(2,1)}, u32[]{:S(2)}) copy-start(bf16[1,1,256,1152]{2,3,1,0:T(8,128)(2,1)} %copy.128) | copy-start | bytes 1769476
  191.3 473.5 %reduce-scatter.4.cloned.1.call-start = ((), (), s32[]{:S(2)}) async-start(), calls=%async_computation.6 | async-start | bytes 368640
  592.4 79.5 %copy-start.1 = (bf16[1152,1152]{1,0:T(8,128)(2,1)S(1)}, bf16[1152,1152]{1,0:T(8,128)(2,1)}, u32[]{:S(2)}) copy-start(bf16[1152,1152]{1,0:T(8,128)(2,1)} %param.21) | copy-start | bytes 7962628
Sparse Core Ops, SparseCore 0:
  584.2 80.5 reduce-scatter.3
where the time goes:
time: 688 us; the launch traced here: 679 us
  blocking collectives  390 us (57%)
  local copies, waits for them, and re-layouts  71.9 us (10%)
  waiting for transfers between devices  70.2 us (10%)
  matrix products  67.8 us (10%)
  starting transfers between devices  53.9 us (8%)
  between operations  15.2 us (2%)
  other arithmetic  9.88 us (1%)
    unnamed x1, blocking collectives  390 us
    unnamed x2, waiting for transfers between devices  70.2 us
    reshape x8, local copies, waits for them, and re-layouts, per_device(): flat = tuple((item.reshape(cell_shape) for item in temporal))  16.4 us
    unnamed x46, local copies, waits for them, and re-layouts  16 us
    mul x1, local copies, waits for them, and re-layouts, per_device(): jnp.stack([part_space, part_time], axis=1) * factor  16 us
    dot_general x2, matrix products, attention_backward(): jnp.einsum('bchlm,bmche->blche', score_grad, keyset, preferred_element_ty...  14.3 us
  transfers between devices with their start and end apart: 6, of which 1 were waited for; matrix products, arithmetic and copies ran while one was open for 20% of the time, Pallas kernels for 0%

commit v1 on v0

v1 whole, which is shorter than its diff:
```python
import functools
import math

import jax
import jax.numpy as jnp
import numpy as np
from jax import lax
from jax.experimental import pallas as pl
from jax.experimental.pallas import tpu as pltpu
from jax.sharding import PartitionSpec as P

HEADS = 16
HEAD_DIM = 72
D = HEADS * HEAD_DIM
CELL = 4
WIN = 256
MESH = pl.DeviceIdType.MESH
F32 = jnp.float32
BF16 = jnp.bfloat16
CHUNK_HEADS = 5


def padded(rows):
    return -(-rows // 16) * 16


def row_maps(n):
    xz, y, c = np.meshgrid(np.arange(n * n), np.arange(n), np.arange(CELL), indexing="ij")
    index = {
        "N": ((xz * n + y) * CELL + c).reshape(-1),
        "C": ((c * n * n + xz) * n + y).reshape(-1),
        "P": ((y * n * n + xz) * CELL + c).reshape(-1),
    }
    tokens = n * n * n * CELL

    def perm(source, target):
        out = np.zeros((tokens, tokens), np.float32)
        out[index[target], index[source]] = 1.0
        return out

    rows_x = D // n
    rows_y = rows_x // n
    rows_z = rows_y // n
    pad_y, pad_z = padded(rows_y), padded(rows_z)
    first = np.zeros((n * pad_y, n * rows_x), np.float32)
    second = np.zeros((n * pad_z, n * pad_y), np.float32)
    third = np.zeros((pad_z, n * pad_z), np.float32)
    for source in range(n):
        for yy in range(n):
            for zz in range(n):
                for r in range(rows_z):
                    first[yy * pad_y + zz * rows_z + r, source * rows_x + (zz * n + yy) * rows_z + r] = 1.0
        for zz in range(n):
            for r in range(rows_z):
                second[zz * pad_z + r, source * pad_y + zz * rows_z + r] = 1.0
        for r in range(rows_z):
            third[r, source * pad_z + r] = 1.0
    made = [perm("N", "P"), perm("P", "C"), perm("N", "C"), perm("C", "P"), perm("P", "N"), first, second, third]
    return [m.astype(jnp.bfloat16) for m in made]


def dot(a, b):
    return lax.dot_general(a, b, (((1,), (0,)), ((), ())), preferred_element_type=F32)


def dot_rows(a, b):
    return lax.dot_general(a, b, (((0,), (0,)), ((), ())), preferred_element_type=F32)


def dot_lanes(a, b):
    return lax.dot_general(a, b, (((1,), (1,)), ((), ())), preferred_element_type=F32)


def head_mask(head, start, width):
    lane = lax.broadcasted_iota(jnp.int32, (1, width), 1) + start
    inside = (lane >= head * HEAD_DIM) & (lane < (head + 1) * HEAD_DIM)
    return jnp.where(inside, 1.0, 0.0).astype(BF16)


def lane_chunks(width, step):
    return [(start, min(step, width - start)) for start in range(0, width, step)]


def permute(matrix, source, target):
    for start, size in lane_chunks(D, 384):
        target[:, start : start + size] = dot(matrix[...], source[:, start : start + size]).astype(BF16)


def project(gated, weight, target):
    def step(i, _):
        at = pl.ds(pl.multiple_of(i * 384, 128), 384)
        target[:, at] = dot_lanes(gated[...], weight[at, :]).astype(BF16)
        return 0

    lax.fori_loop(0, D // 384, step, 0)


def softmax_and_grad(scores, grads):
    factor = math.log2(math.e) / math.sqrt(HEAD_DIM)
    highest = jnp.max(scores, axis=0, keepdims=True)
    raised = jnp.exp2((scores - highest) * factor)
    shares = raised * (1.0 / jnp.sum(raised, axis=0, keepdims=True))
    centre = jnp.sum(shares * grads, axis=0, keepdims=True)
    return shares.astype(BF16), (shares * (grads - centre)).astype(BF16)


def window(head):
    start = jnp.minimum(head * HEAD_DIM // 128, (D - WIN) // 128) * 128
    return pl.multiple_of(start, 128)


def scores_space(q, k, v, u, shares, grads):
    def step(head, _):
        start = window(head)
        at = pl.ds(start, WIN)
        mask = head_mask(head, start, WIN)
        scores = dot_lanes(k[:, at] * mask, q[:, at])
        share_grad = dot_lanes(v[:, at] * mask, u[:, at])
        shares[head], grads[head] = softmax_and_grad(scores, share_grad)
        return 0

    lax.fori_loop(0, HEADS, step, 0)


def scores_time(q, k, v, u, shares, grads):
    tokens = q.shape[0]
    half, frames = tokens // 2, tokens // CELL
    lane = lax.broadcasted_iota(jnp.int32, (1, half), 1)
    low = lane < frames
    cell_of_lane = lax.broadcasted_iota(jnp.int32, (1, tokens), 1) // frames

    def compact(a, b):
        parts = []
        for i in range(2):
            rows = slice(i * half, (i + 1) * half)
            block = dot_lanes(a[rows, :], b[rows, :])
            parts.append(jnp.where(low, block[:frames, :], block[frames:, :]))
        return jnp.concatenate(parts, axis=1)

    def expand(block):
        zero = jnp.zeros_like(block)
        return jnp.concatenate([jnp.where(cell_of_lane == c, block, zero) for c in range(CELL)], axis=0)

    def step(head, _):
        start = window(head)
        at = pl.ds(start, WIN)
        mask = head_mask(head, start, WIN)
        scores = compact(k[:, at] * mask, q[:, at])
        share_grad = compact(v[:, at] * mask, u[:, at])
        share, grad = softmax_and_grad(scores, share_grad)
        shares[head] = expand(share)
        grads[head] = expand(grad)
        return 0

    lax.fori_loop(0, HEADS, step, 0)


def gradients(q, k, v, u, shares, grads, attended, dq, dk, dv):
    factor = 1.0 / math.sqrt(HEAD_DIM)

    def chunk(first, heads, start, width):
        at = pl.ds(start, width)
        totals = [None] * 4
        for i in range(heads):
            head = first + i
            mask = head_mask(head, start, width)
            terms = (
                dot_rows(shares[head], v[:, at] * mask),
                dot_rows(grads[head], k[:, at] * mask),
                dot(grads[head], q[:, at] * mask),
                dot(shares[head], u[:, at] * mask),
            )
            totals = [term if total is None else total + term for total, term in zip(totals, terms)]
        attended[:, at] = totals[0].astype(BF16)
        dq[:, at] = (totals[1] * factor).astype(BF16)
        dk[:, at] = (totals[2] * factor).astype(BF16)
        dv[:, at] = totals[3].astype(BF16)

    def step(i, _):
        start = pl.multiple_of(i * WIN, 128)
        chunk(start // HEAD_DIM, CHUNK_HEADS, start, WIN)
        return 0

    whole = D // WIN
    lax.fori_loop(0, whole, step, 0)
    tail = whole * WIN
    chunk(tail // HEAD_DIM, HEADS - tail // HEAD_DIM, tail, D - tail)


def kernel(
    n,
    tokens_total,
    qs_h,
    ks_h,
    vs_h,
    qt_h,
    kt_h,
    vt_h,
    cot_h,
    ws_h,
    wt_h,
    np_h,
    pc_h,
    nc_h,
    cp_h,
    pn_h,
    first_h,
    second_h,
    third_h,
    gate_s,
    gate_t,
    dqs_o,
    dks_o,
    dvs_o,
    dqt_o,
    dkt_o,
    dvt_o,
    gws_o,
    gwt_o,
    qs,
    ks,
    vs,
    qraw,
    kraw,
    vraw,
    cot,
    ws,
    wt,
    m_np,
    m_pc,
    m_nc,
    m_cp,
    m_pn,
    m_first,
    m_second,
    m_third,
    wide,
    qt,
    kt,
    vt,
    rc1,
    mid,
    rc2,
    cot_c,
    gated,
    attended,
    up,
    shares,
    grads,
    spatial,
    temporal,
    sent,
    got_y,
    turned,
    far_a,
    far_g,
    product,
    got_x,
    send_y,
    got_wy,
    send_z,
    got_wz,
    send_h,
    got_h,
    send_c,
    got_c,
    load_sem,
    store_sem,
    own_sem,
    c1_send,
    c1_recv,
    c2_send,
    c2_recv,
    ty_send,
    ty_recv,
    tx_send,
    tx_recv,
    w_send,
    w_recv,
    pair_send,
    pair_recv,
):
    dp = lax.axis_index("dp")
    seq = lax.axis_index("seq")
    groups = n * n
    group, y = seq // n, seq % n
    x, z = group // n, group % n
    core = dp % 2
    sibling = dp + 1 - 2 * core
    partner = (dp + 2) % 4
    rows_g = n * CELL
    rows_y = groups * CELL

    loads = [
        pltpu.make_async_copy(source, target, load_sem.at[i])
        for i, (source, target) in enumerate(
            (
                (cot_h, cot),
                (ws_h, ws),
                (qs_h, qs),
                (ks_h, ks),
                (vs_h, vs),
                (qt_h, qraw),
                (kt_h, kraw),
                (vt_h, vraw),
                (wt_h, wt),
                (np_h, m_np),
                (pc_h, m_pc),
                (nc_h, m_nc),
                (cp_h, m_cp),
                (pn_h, m_pn),
                (first_h, m_first),
                (second_h, m_second),
                (third_h, m_third),
            )
        )
    ]
    for load in loads:
        load.start()

    def group_peer(g):
        return (dp, g * n + y)

    def y_peer(yy):
        return (dp, group * n + yy)

    def x_peer(xx):
        return (dp, (xx * n + z) * n + y)

    def z_peer(zz):
        return (dp, (x * n + zz) * n + y)

    barrier = pltpu.get_barrier_semaphore()

    def greet(device):
        pl.semaphore_signal(barrier, inc=1, device_id=device, device_id_type=MESH)

    def greet_group(i, _):
        greet(group_peer((group + i) % groups))
        return 0

    lax.fori_loop(1, groups, greet_group, 0)
    for i in range(1, n):
        greet(y_peer((y + i) % n))
    greet((sibling, seq))
    greet((partner, seq))
    pl.semaphore_wait(barrier, groups - 1 + n - 1 + 2)

    def exchange(size, me, device, source, target, send, recv):
        def copy(i):
            peer = (me + i) % size
            return pltpu.make_async_remote_copy(
                src_ref=source(peer),
                dst_ref=target(me),
                send_sem=send(i),
                recv_sem=recv(i),
                device_id=device(peer),
                device_id_type=MESH,
            )

        def start():
            def step(i, _):
                copy(i).start()
                return 0

            lax.fori_loop(1, size, step, 0)

        def wait_recv():
            def step(i, _):
                copy(i).wait_recv()
                return 0

            lax.fori_loop(1, size, step, 0)

        def wait_send():
            def step(i, _):
                copy(i).wait_send()
                return 0

            lax.fori_loop(1, size, step, 0)

        return start, wait_recv, wait_send

    def rows(ref, at, count):
        return ref.at[pl.ds(pl.multiple_of(at * count, 16 if count % 16 == 0 else 8), count)]

    sends = []

    loads[0].wait()
    c1_start, c1_wait, c1_done = exchange(
        groups,
        group,
        group_peer,
        lambda g: rows(cot, g, rows_g),
        lambda g: rows(rc1, g, rows_g),
        lambda i: c1_send.at[i],
        lambda i: c1_recv.at[i],
    )
    c1_start()
    sends.append(c1_done)
    own1 = pltpu.make_async_copy(rows(cot, group, rows_g), rows(rc1, group, rows_g), own_sem.at[0])
    own1.start()

    gated[0] = (gate_s[...] * cot[...].astype(F32)).astype(BF16)
    loads[1].wait()
    project(gated.at[0], ws, up)
    for load in loads[2:5]:
        load.wait()
    scores_space(qs, ks, vs, up, shares, grads)

    loads[11].wait()
    for raw, target, load in ((qraw, qt, loads[5]), (kraw, kt, loads[6]), (vraw, vt, loads[7])):
        load.wait()

        def widen(i, _):
            pair = jnp.concatenate([raw[2 * i].astype(F32), raw[2 * i + 1].astype(F32)], axis=0)
            wide[pl.ds(pl.multiple_of(i * 8, 8), 8), :] = pair
            return 0

        lax.fori_loop(0, raw.shape[0] // 2, widen, 0)
        for start, size in lane_chunks(D, 384):
            part = wide[:, start : start + size].astype(BF16)
            target[:, start : start + size] = dot(m_nc[...], part).astype(BF16)

    own1.wait()
    c1_wait()
    loads[9].wait()
    permute(m_np, rc1, mid)
    c2_start, c2_wait, c2_done = exchange(
        n,
        y,
        y_peer,
        lambda yy: rows(mid, yy, rows_y),
        lambda yy: rows(rc2, yy, rows_y),
        lambda i: c2_send.at[i],
        lambda i: c2_recv.at[i],
    )
    c2_start()
    sends.append(c2_done)
    own2 = pltpu.make_async_copy(rows(mid, y, rows_y), rows(rc2, y, rows_y), own_sem.at[1])
    own2.start()

    gradients(qs, ks, vs, up, shares, grads, attended.at[0], spatial.at[0], spatial.at[1], spatial.at[2])
    stores = [
        pltpu.make_async_copy(spatial.at[i], out, store_sem.at[i]) for i, out in enumerate((dqs_o, dks_o, dvs_o))
    ]
    for store in stores:
        store.start()

    own2.wait()
    c2_wait()
    loads[10].wait()
    permute(m_pc, rc2, cot_c)
    gated[1] = (gate_t[...] * cot_c[...].astype(F32)).astype(BF16)
    loads[8].wait()
    project(gated.at[1], wt, up)
    scores_time(qt, kt, vt, up, shares, grads)
    gradients(qt, kt, vt, up, shares, grads, attended.at[1], temporal.at[0], temporal.at[1], temporal.at[2])

    loads[12].wait()
    outs = (dqt_o, dkt_o, dvt_o)
    first_steps = []
    for i in range(3):
        permute(m_cp, temporal.at[i], sent.at[i])
        start, wait, done = exchange(
            n,
            y,
            y_peer,
            lambda yy, i=i: rows(sent.at[i], yy, rows_y),
            lambda yy, i=i: rows(got_y.at[i], yy, rows_y),
            lambda k, i=i: ty_send.at[i * n + k],
            lambda k, i=i: ty_recv.at[i * n + k],
        )
        start()
        sends.append(done)
        own = pltpu.make_async_copy(rows(sent.at[i], y, rows_y), rows(got_y.at[i], y, rows_y), own_sem.at[2 + i])
        own.start()
        first_steps.append((own, wait))

    pair = [
        pltpu.make_async_remote_copy(
            src_ref=source.at[1 - core],
            dst_ref=target,
            send_sem=pair_send.at[i],
            recv_sem=pair_recv.at[i],
            device_id=(sibling, seq),
            device_id_type=MESH,
        )
        for i, (source, target) in enumerate(((attended, far_a), (gated, far_g)))
    ]
    for copy in pair:
        copy.start()

    loads[13].wait()
    last_steps = []
    for i in range(3):
        own, wait = first_steps[i]
        own.wait()
        wait()
        permute(m_pn, got_y.at[i], turned.at[i])
        start, wait, done = exchange(
            groups,
            group,
            group_peer,
            lambda g, i=i: rows(turned.at[i], g, rows_g),
            lambda g, i=i: rows(outs[i], g, rows_g),
            lambda k, i=i: tx_send.at[i * groups + k],
            lambda k, i=i: tx_recv.at[i * groups + k],
        )
        start()
        sends.append(done)
        own = pltpu.make_async_copy(rows(turned.at[i], group, rows_g), rows(outs[i], group, rows_g), own_sem.at[5 + i])
        own.start()
        last_steps.append((own, wait))

    for copy in pair:
        copy.wait_recv()
    scale = 1.0 / math.sqrt(tokens_total)

    def multiply(i, _):
        at = pl.ds(pl.multiple_of(i * 128, 128), 128)
        near, far = attended[core, :, at], far_a[:, at]
        for start, size in lane_chunks(D, 384):
            to = slice(start, start + size)
            total = dot_rows(near, gated[core, :, to]) + dot_rows(far, far_g[:, to])
            product[at, to] = (total * scale).astype(BF16)
        return 0

    lax.fori_loop(0, D // 128, multiply, 0)

    def reduce(size, me, device, source, target, slot, matrix, result, own):
        count = target.shape[0] // size
        start, wait, done = exchange(
            size,
            me,
            device,
            lambda peer: rows(source, peer, count),
            lambda peer: rows(target, peer, count),
            lambda k: w_send.at[slot * n + k],
            lambda k: w_recv.at[slot * n + k],
        )
        start()
        sends.append(done)
        near = pltpu.make_async_copy(rows(source, me, count), rows(target, me, count), own)
        near.start()
        near.wait()
        wait()
        for at, width in lane_chunks(D, 384):
            result[:, at : at + width] = dot(matrix[...], target[:, at : at + width]).astype(BF16)

    for load in loads[14:]:
        load.wait()
    reduce(n, x, x_peer, product, got_x, 0, m_first, send_y, own_sem.at[8])
    reduce(n, y, y_peer, send_y, got_wy, 1, m_second, send_z, own_sem.at[9])
    reduce(n, z, z_peer, send_z, got_wz, 2, m_third, send_h, own_sem.at[10])

    def swap(source, target, slot, device):
        copy = pltpu.make_async_remote_copy(
            src_ref=source,
            dst_ref=target,
            send_sem=pair_send.at[slot],
            recv_sem=pair_recv.at[slot],
            device_id=device,
            device_id_type=MESH,
        )
        copy.start()
        copy.wait_recv()
        return copy

    pair.append(swap(send_h, got_h, 2, (partner, seq)))
    send_c[...] = (send_h[...].astype(F32) + got_h[...].astype(F32)).astype(BF16)
    pair.append(swap(send_c, got_c, 3, (sibling, seq)))
    count, width = gws_o.shape
    for i in range(4):

        @pl.when(dp == i)
        def _():
            at = slice(i * width, (i + 1) * width)
            near = send_c[...].astype(F32)[:count, at]
            far = got_c[...].astype(F32)[:count, at]
            gws_o[...] = far if i % 2 else near
            gwt_o[...] = near if i % 2 else far

    for own, wait in last_steps:
        own.wait()
        wait()
    for store in stores:
        store.wait()
    for done in sends:
        done()
    for copy in pair:
        copy.wait_send()


def per_device(n, maps, qs, ks, vs, qt, kt, vt, cot, gate_s, gate_t, ws, wt):
    tokens = cot.shape[2]
    frames = qt.shape[1]
    groups = n * n
    pad_y, pad_z = padded(D // n // n), padded(D // n // n // n)
    shape = cot.shape
    flat = lambda a: a.reshape(tokens, D)
    cells = lambda a: a.reshape(frames, CELL, D)
    any_space = pl.BlockSpec(memory_space=pl.ANY)
    vmem = pl.BlockSpec(memory_space=pltpu.VMEM)
    token = pltpu.VMEM((tokens, D), BF16)
    tokens_of = lambda k: pltpu.VMEM((k, tokens, D), BF16)
    square = pltpu.VMEM((tokens, tokens), BF16)
    raw = pltpu.VMEM((frames, CELL, D), BF16)
    weight = pltpu.VMEM((D, D), BF16)
    dma = lambda k: pltpu.SemaphoreType.DMA((k,))
    small = pltpu.VMEM((pad_z, D), BF16)
    total = 4 * n**3 * tokens
    out_rows, out_columns = D // n**3, D // 4
    result = pl.pallas_call(
        functools.partial(kernel, n, total),
        out_shape=[jax.ShapeDtypeStruct((tokens, D), BF16)] * 6
        + [jax.ShapeDtypeStruct((out_rows, out_columns), F32)] * 2,
        in_specs=[any_space] * 17 + [vmem] * 2,
        out_specs=[any_space] * 6 + [vmem] * 2,
        scratch_shapes=[token] * 3
        + [raw] * 3
        + [token]
        + [weight] * 2
        + [square] * 5
        + [pltpu.VMEM(m.shape, BF16) for m in maps[5:]]
        + [pltpu.VMEM((tokens, D), F32)]
        + [token] * 3
        + [token] * 4
        + [tokens_of(2)] * 2
        + [token]
        + [pltpu.VMEM((HEADS, tokens, tokens), BF16)] * 2
        + [tokens_of(3)] * 5
        + [token] * 2
        + [weight] * 2
        + [pltpu.VMEM((n * pad_y, D), BF16)] * 2
        + [pltpu.VMEM((n * pad_z, D), BF16)] * 2
        + [small] * 4
        + [dma(17), dma(3), dma(11)]
        + [dma(groups)] * 2
        + [dma(n)] * 2
        + [dma(3 * n)] * 2
        + [dma(3 * groups)] * 2
        + [dma(3 * n)] * 2
        + [dma(4)] * 2,
        compiler_params=pltpu.CompilerParams(
            collective_id=0, has_side_effects=True, vmem_limit_bytes=60 * 1024 * 1024
        ),
    )(flat(qs), flat(ks), flat(vs), cells(qt), cells(kt), cells(vt), flat(cot), ws, wt, *maps, gate_s, gate_t)
    return tuple(a.reshape(shape) for a in result[:6]) + tuple(result[6:])


def solution(mesh):
    n = round(mesh.shape["seq"] ** (1 / 3))
    maps = row_maps(n)
    frames = P("dp", "seq", None, None)
    cells = P("dp", None, "seq", None)

    def run(*args):
        return per_device(n, [jnp.asarray(m) for m in maps], *args)

    return jax.shard_map(
        run,
        mesh=mesh,
        in_specs=(frames,) * 3 + (cells,) * 3 + (frames, P("dp", None), P("dp", None), P(), P()),
        out_specs=(frames,) * 6 + (P("seq", "dp"),) * 2,
        check_vma=False,
    )
```

time: 688 us -> 145 us (0.21); the launches traced: 679 us -> 144 us
  blocking collectives: 390 us -> 0 us
  Pallas kernels: 0 us -> 134 us
  waiting for transfers between devices: 70.2 us -> 0 us
  matrix products: 67.8 us -> 0 us
  local copies, waits for them, and re-layouts: 71.9 us -> 8.55 us
  starting transfers between devices: 53.9 us -> 0 us
  between operations: 15.2 us -> 0.68 us
  other arithmetic: 9.88 us -> 0 us
    unnamed x1 -> x0, blocking collectives: 390 us -> none
    pallas_call x0 -> x1, Pallas kernels: none -> 134 us  [per_device(): pl.pallas_call(functools.partial(kernel, n, total), out_shape=[jax.ShapeD...]
    unnamed x2 -> x0, waiting for transfers between devices: 70.2 us -> none
    dot_general x14 -> x0, matrix products: 58.3 us -> none  [the longest x2 14.3 us: attention_backward(): jnp.einsum('bchlm,bmche->blche', score_grad, keyset, preferred_element_ty...]
    all_to_all x5 -> x0, starting transfers between devices: 53.9 us -> none  [the longest x1 12.7 us: per_device(): lax.all_to_all(upstream_time, 'seq', split_axis=2, concat_axis=1, tiled=T...]
    reshape x10 -> x0, local copies, waits for them, and re-layouts: 18.8 us -> none  [the longest x8 16.4 us: per_device(): flat = tuple((item.reshape(cell_shape) for item in temporal))]
    mul x1 -> x0, local copies, waits for them, and re-layouts: 16 us -> none  [per_device(): jnp.stack([part_space, part_time], axis=1) * factor]
    another operation x4 -> x0, local copies, waits for them, and re-layouts: 10.6 us -> none
  transfers between devices with their start and end apart: 6 -> 0, of which waited for: 1 -> 0; matrix products, arithmetic and copies ran while one was open for 20% -> 0% of each run, Pallas kernels for 0% -> 0%
where the time goes in v1:
time: 145 us; the launch traced here: 144 us
  Pallas kernels  134 us (92%)
  local copies, waits for them, and re-layouts  8.55 us (6%)
    pallas_call x1, Pallas kernels, per_device(): pl.pallas_call(functools.partial(kernel, n, total), out_shape=[jax.ShapeD...  134 us
    unnamed x20, local copies, waits for them, and re-layouts  8.55 us

profile of v1, /device:TPU:1, one launch (start us, length us, event | category | flops | bytes accessed | tf_op | source)
XLA Modules:
  0.0 143.7 jit_solution(17636881565247173875)
XLA Ops:
  0.6 134.5 %shard_map.242 = (bf16[256,1152]{1,0:T(8,128)(2,1)}, bf16[256,1152]{1,0:T(8,128)(2,1)}, bf16[256,1152]{1,0:T(8,128)(2,1)}, bf16[256,1152]{1,0:T(8,128)(2,1)}, bf...) custom-call(bf16[256,1152]{1,0:T(8,128)(2,1)} %bitcast.13, ...), custom_call_target="tpu_custom_call" | custom-call | tf_op jit(solution)/shard_map/pallas_call | solution.py:614
  135.1 0.0 copy-start.3
  135.1 0.0 copy-start.2
  135.1 0.0 copy-start.1
  135.1 2.0 %copy.35 = bf16[1,1,256,1152]{3,2,1,0:T(8,128)(2,1)} copy(bf16[1,1,256,1152]{3,2,1,0:T(8,128)(2,1)} %bitcast.25) | data formatting | bytes 1179648
  137.2 0.0 copy-start
  137.2 2.0 %copy.36 = bf16[1,1,256,1152]{3,2,1,0:T(8,128)(2,1)} copy(bf16[1,1,256,1152]{3,2,1,0:T(8,128)(2,1)} %bitcast.24) | data formatting | bytes 1179648
  139.2 0.0 copy-done.3
  139.2 0.0 copy-start.5
  139.2 0.0 copy-start.4
  139.2 0.8 copy.37
  140.0 0.0 copy-done.2
  140.0 0.8 copy.38
  140.8 0.0 copy-done.1
  140.8 0.8 copy.39
  141.6 0.0 copy-done
  141.6 0.8 copy.40
  142.5 0.0 copy-done.5
  142.5 0.6 copy.41
  143.1 0.0 copy-done.4
  143.1 0.6 copy.42
Async XLA Ops:
  135.1 4.1 %copy-start.3 = (bf16[256,1152]{1,0:T(8,128)(2,1)S(1)}, bf16[256,1152]{1,0:T(8,128)(2,1)}, u32[]{:S(2)}) copy-start(bf16[256,1152]{1,0:T(8,128)(2,1)} %get-tuple-element.18) | copy-start | bytes 1769476
  135.1 4.9 %copy-start.2 = (bf16[256,1152]{1,0:T(8,128)(2,1)S(1)}, bf16[256,1152]{1,0:T(8,128)(2,1)}, u32[]{:S(2)}) copy-start(bf16[256,1152]{1,0:T(8,128)(2,1)} %get-tuple-element.19) | copy-start | bytes 1769476
  135.1 5.7 %copy-start.1 = (bf16[256,1152]{1,0:T(8,128)(2,1)S(1)}, bf16[256,1152]{1,0:T(8,128)(2,1)}, u32[]{:S(2)}) copy-start(bf16[256,1152]{1,0:T(8,128)(2,1)} %get-tuple-element.20) | copy-start | bytes 1769476
  137.2 4.4 %copy-start = (bf16[256,1152]{1,0:T(8,128)(2,1)S(1)}, bf16[256,1152]{1,0:T(8,128)(2,1)}, u32[]{:S(2)}) copy-start(bf16[256,1152]{1,0:T(8,128)(2,1)} %get-tuple-element.21) | copy-start | bytes 1769476
  139.2 3.3 %copy-start.5 = (f32[18,288]{1,0:T(8,128)S(1)}, f32[18,288]{1,0:T(8,128)}, u32[]{:S(2)}) copy-start(f32[18,288]{1,0:T(8,128)} %get-tuple-element.38) | copy-start | bytes 62212
  139.2 3.9 %copy-start.4 = (f32[18,288]{1,0:T(8,128)S(1)}, f32[18,288]{1,0:T(8,128)}, u32[]{:S(2)}) copy-start(f32[18,288]{1,0:T(8,128)} %get-tuple-element.39) | copy-start | bytes 62212

commit v2 on v0

v2 whole, which is shorter than its diff:
```python
import functools
import math

import jax
import jax.numpy as jnp
import numpy as np
from jax import lax
from jax.experimental import pallas as pl
from jax.experimental.pallas import tpu as pltpu
from jax.sharding import PartitionSpec as P

HEADS = 16
HEAD_DIM = 72
D = HEADS * HEAD_DIM
CELL = 4
WIN = 256
MESH = pl.DeviceIdType.MESH
F32 = jnp.float32
BF16 = jnp.bfloat16
CHUNK_HEADS = 5


def padded(rows):
    return -(-rows // 16) * 16


def row_maps(n):
    rows_x = D // n
    rows_y = rows_x // n
    rows_z = rows_y // n
    pad_y, pad_z = padded(rows_y), padded(rows_z)
    turn = np.zeros((D, D), np.float32)
    first_x = np.zeros((n * pad_y, D), np.float32)
    first_y = np.zeros((n * pad_y, D), np.float32)
    second = np.zeros((n * pad_z, n * pad_y), np.float32)
    r = np.arange(rows_z)
    for i in range(n):
        for zz in range(n):
            for j in range(n):
                turn[((j * n + i) * n + zz) * rows_z + r, ((i * n + zz) * n + j) * rows_z + r] = 1.0
                first_x[j * pad_y + zz * rows_z + r, i * rows_x + (zz * n + j) * rows_z + r] = 1.0
                first_y[j * pad_y + zz * rows_z + r, i * rows_x + (j * n + zz) * rows_z + r] = 1.0
            second[zz * pad_z + r, i * pad_y + zz * rows_z + r] = 1.0
    return [m.astype(jnp.bfloat16) for m in (turn, first_x, first_y, second)]


def dot(a, b):
    return lax.dot_general(a, b, (((1,), (0,)), ((), ())), preferred_element_type=F32)


def dot_rows(a, b):
    return lax.dot_general(a, b, (((0,), (0,)), ((), ())), preferred_element_type=F32)


def dot_lanes(a, b):
    return lax.dot_general(a, b, (((1,), (1,)), ((), ())), preferred_element_type=F32)


def head_mask(head, start, width):
    lane = lax.broadcasted_iota(jnp.int32, (1, width), 1) + start
    inside = (lane >= head * HEAD_DIM) & (lane < (head + 1) * HEAD_DIM)
    return jnp.where(inside, 1.0, 0.0).astype(BF16)


def lane_chunks(width, step):
    return [(start, min(step, width - start)) for start in range(0, width, step)]


def project(gated, weight, target, start, width):
    at = pl.ds(start, width)
    target[:, at] = dot_lanes(gated[...], weight[at, :]).astype(BF16)


def softmax_and_grad(scores, grads):
    factor = math.log2(math.e) / math.sqrt(HEAD_DIM)
    highest = jnp.max(scores, axis=0, keepdims=True)
    raised = jnp.exp2((scores - highest) * factor)
    shares = raised * (1.0 / jnp.sum(raised, axis=0, keepdims=True))
    centre = jnp.sum(shares * grads, axis=0, keepdims=True)
    return shares.astype(BF16), (shares * (grads - centre)).astype(BF16)


def window(head):
    start = jnp.minimum(head * HEAD_DIM // 128, (D - WIN) // 128) * 128
    return pl.multiple_of(start, 128)


def scores_space(q, k, v, u, shares, grads):
    def step(head, _):
        start = window(head)
        at = pl.ds(start, WIN)
        mask = head_mask(head, start, WIN)
        scores = dot_lanes(k[:, at] * mask, q[:, at])
        share_grad = dot_lanes(v[:, at] * mask, u[:, at])
        shares[head], grads[head] = softmax_and_grad(scores, share_grad)
        return 0

    lax.fori_loop(0, HEADS, step, 0, unroll=4)


def score_time(head, q, k, v, u, shares, grads):
    tokens = q.shape[0]
    half, frames = tokens // 2, tokens // CELL
    low = lax.broadcasted_iota(jnp.int32, (1, half), 1) < frames
    cell_of_lane = lax.broadcasted_iota(jnp.int32, (1, tokens), 1) // frames
    start = window(head)
    at = pl.ds(start, WIN)
    mask = head_mask(head, start, WIN)

    def compact(a, b):
        parts = []
        for i in range(2):
            rows = slice(i * half, (i + 1) * half)
            block = dot_lanes(a[rows, :], b[rows, :])
            parts.append(jnp.where(low, block[:frames, :], block[frames:, :]))
        return jnp.concatenate(parts, axis=1)

    def expand(block):
        zero = jnp.zeros_like(block)
        return jnp.concatenate([jnp.where(cell_of_lane == c, block, zero) for c in range(CELL)], axis=0)

    scores = compact(k[:, at] * mask, q[:, at])
    share_grad = compact(v[:, at] * mask, u[:, at])
    share, grad = softmax_and_grad(scores, share_grad)
    shares[head] = expand(share)
    grads[head] = expand(grad)


def gradients(first, heads, start, width, q, k, v, u, shares, grads):
    factor = 1.0 / math.sqrt(HEAD_DIM)
    at = pl.ds(start, width)
    totals = [None] * 4
    for i in range(heads):
        head = first + i
        mask = head_mask(head, start, width)
        terms = (
            dot_rows(shares[head], v[:, at] * mask),
            dot_rows(grads[head], k[:, at] * mask),
            dot(grads[head], q[:, at] * mask),
            dot(shares[head], u[:, at] * mask),
        )
        totals = [term if total is None else total + term for total, term in zip(totals, terms)]
    return totals[0], totals[1] * factor, totals[2] * factor, totals[3]


def to_slabs(source, target, count):
    def step(i, _):
        wide = source[pl.ds(pl.multiple_of(i * 16, 16), 16), :].astype(F32)
        for j in range(16 // CELL):
            target[i * (16 // CELL) + j] = wide[j * CELL : (j + 1) * CELL, :].astype(BF16)
        return 0

    lax.fori_loop(0, count * CELL // 16, step, 0, unroll=2)


def slabs_to_cells(source, wide):
    frames = source.shape[0]

    def step(f, _):
        slab = source[f].astype(F32)
        for t in range(D // 128):
            wide[t, pl.ds(f, CELL, stride=frames), :] = slab[:, t * 128 : (t + 1) * 128]
        return 0

    lax.fori_loop(0, frames, step, 0, unroll=8)


def kernel(
    n,
    tokens_total,
    qs_h,
    ks_h,
    vs_h,
    qt_h,
    kt_h,
    vt_h,
    cot_h,
    ws_h,
    wt_h,
    turn_h,
    first_x_h,
    first_y_h,
    second_h,
    gate_s,
    gate_t,
    dqs_o,
    dks_o,
    dvs_o,
    dqt_o,
    dkt_o,
    dvt_o,
    gws_o,
    gwt_o,
    qs,
    ks,
    vs,
    qraw,
    kraw,
    vraw,
    cot,
    ws,
    wt,
    turn,
    first_x,
    first_y,
    second,
    wide,
    parts,
    qt,
    kt,
    vt,
    cot_slabs,
    cot_got,
    gated,
    attended,
    up,
    shares,
    grads,
    spatial,
    temporal,
    sent,
    got,
    far_a,
    far_g,
    product,
    turned,
    got_1x,
    got_1y,
    send_2x,
    send_2y,
    got_2x,
    got_2y,
    send_z,
    got_z,
    send_h,
    got_h,
    send_c,
    got_c,
    load_sem,
    store_sem,
    own_sem,
    cot_send,
    cot_recv,
    t_send,
    t_recv,
    w_send,
    w_recv,
    pair_send,
    pair_recv,
):
    dp = lax.axis_index("dp")
    seq = lax.axis_index("seq")
    devices = n * n * n
    group, y = seq // n, seq % n
    x, z = group // n, group % n
    core, side = dp % 2, dp // 2
    sibling = dp + 1 - 2 * core
    partner = (dp + 2) % 4
    tokens = devices * CELL
    split = product.shape[1] - got_1y.shape[1]

    loads = [
        pltpu.make_async_copy(source, target, load_sem.at[i])
        for i, (source, target) in enumerate(
            (
                (cot_h, cot),
                (ws_h, ws),
                (qs_h, qs),
                (ks_h, ks),
                (vs_h, vs),
                (qt_h, qraw),
                (kt_h, kraw),
                (vt_h, vraw),
                (wt_h, wt),
                (turn_h, turn),
                (first_x_h, first_x),
                (first_y_h, first_y),
                (second_h, second),
            )
        )
    ]
    for load in loads:
        load.start()

    def seq_peer(s):
        return (dp, s)

    def y_peer(yy):
        return (dp, group * n + yy)

    def x_peer(xx):
        return (dp, (xx * n + z) * n + y)

    def z_peer(zz):
        return (dp, (x * n + zz) * n + y)

    barrier = pltpu.get_barrier_semaphore()

    def greet(device):
        pl.semaphore_signal(barrier, inc=1, device_id=device, device_id_type=MESH)

    def greet_seq(i, _):
        greet(seq_peer((seq + i) % devices))
        return 0

    lax.fori_loop(1, devices, greet_seq, 0)
    greet((sibling, seq))
    greet((partner, seq))
    loads[0].wait()
    to_slabs(cot, cot_slabs, devices)
    pl.semaphore_wait(barrier, devices - 1 + 2)

    def remote(source, target, send, recv, device):
        return pltpu.make_async_remote_copy(
            src_ref=source,
            dst_ref=target,
            send_sem=send,
            recv_sem=recv,
            device_id=device,
            device_id_type=MESH,
        )

    def local(source, target, sem):
        return pltpu.make_async_copy(source, target, sem)

    def send_cot(i, _):
        peer = (seq + i) % devices
        remote(cot_slabs.at[peer], cot_got.at[seq], cot_send.at[0], cot_recv.at[0], seq_peer(peer)).start()
        return 0

    lax.fori_loop(1, devices, send_cot, 0)
    cot_own = local(cot_slabs.at[seq], cot_got.at[seq], own_sem.at[0])
    cot_own.start()

    gated[0] = (gate_s[...] * cot[...].astype(F32)).astype(BF16)
    loads[1].wait()
    for start, width in lane_chunks(D, 384):
        project(gated.at[0], ws, up, start, width)
    for load in loads[2:5]:
        load.wait()
    scores_space(qs, ks, vs, up, shares, grads)
    whole = D // WIN
    tail = whole * WIN

    def space_window(first, heads, start, width):
        at = pl.ds(start, width)
        total = gradients(first, heads, start, width, qs, ks, vs, up, shares, grads)
        attended[0, :, at] = total[0].astype(BF16)
        for i in range(3):
            spatial[i, :, at] = total[1 + i].astype(BF16)

    def space_step(i, _):
        start = pl.multiple_of(i * WIN, 128)
        space_window(start // HEAD_DIM, CHUNK_HEADS, start, WIN)
        return 0

    lax.fori_loop(0, whole, space_step, 0)
    space_window(tail // HEAD_DIM, HEADS - tail // HEAD_DIM, tail, D - tail)

    def pair_copies(kind):
        return [
            remote(source.at[kind], target, pair_send.at[i], pair_recv.at[i], (sibling, seq))
            for i, (source, target) in enumerate(((attended, far_a), (gated, far_g)))
        ]

    @pl.when(core == 1)
    def _():
        for copy in pair_copies(0):
            copy.start()

    stores = [local(spatial.at[i], out, store_sem.at[i]) for i, out in enumerate((dqs_o, dks_o, dvs_o))]
    for store in stores:
        store.start()

    for raw, target, load in ((qraw, qt, loads[5]), (kraw, kt, loads[6]), (vraw, vt, loads[7])):
        load.wait()
        slabs_to_cells(raw, wide)
        for t in range(D // 128):
            target[:, t * 128 : (t + 1) * 128] = wide[t].astype(BF16)

    def rows(ref, at, count):
        return ref.at[pl.ds(pl.multiple_of(at * count, 16 if count % 16 == 0 else 8), count)]

    def exchange(me, device, source, target, slot):
        copies = []
        for i in range(1, n):
            peer = (me + i) % n
            k = slot * n + i
            copies.append(remote(source(peer), target(me), w_send.at[k], w_recv.at[k], device(peer)))
        own = local(source(me), target(me), own_sem.at[1 + slot])
        return own, copies

    count_1, count_2 = D // n, send_2x.shape[0] // n
    lanes_1 = slice(0, split)
    steps = (
        exchange(x, x_peer, lambda p: rows(product, p, count_1).at[:, lanes_1], lambda p: rows(got_1x, p, count_1), 0),
        exchange(y, y_peer, lambda p: rows(turned, p, count_1), lambda p: rows(got_1y, p, count_1), 1),
        exchange(y, y_peer, lambda p: rows(send_2x, p, count_2), lambda p: rows(got_2x, p, count_2), 2),
        exchange(x, x_peer, lambda p: rows(send_2y, p, count_2), lambda p: rows(got_2y, p, count_2), 3),
        exchange(z, z_peer, lambda p: send_z.at[p], lambda p: got_z.at[p], 4),
    )

    def begin(step):
        own, copies = step
        for copy in copies:
            copy.start()
        own.start()

    def arrived(step):
        own, copies = step
        own.wait()
        for copy in copies:
            copy.wait_recv()

    scale = 1.0 / math.sqrt(tokens_total)

    def weight_product():
        for copy in pair_copies(0):
            copy.wait_recv()

        def multiply(start, width):
            to = slice(start, start + width)

            def step(i, _):
                at = pl.ds(pl.multiple_of(i * 128, 128), 128)
                total = dot_rows(attended[core, :, at], gated[core, :, to]) + dot_rows(far_a[:, at], far_g[:, to])
                product[at, to] = (total * scale).astype(BF16)
                return 0

            lax.fori_loop(0, D // 128, step, 0, unroll=3)

        multiply(0, split)
        begin(steps[0])
        multiply(split, D - split)
        loads[9].wait()

        def turn_rows(i, _):
            at = pl.ds(pl.multiple_of(i * 128, 128), 128)
            turned[at, :] = dot(turn[at, :], product[:, split:]).astype(BF16)
            return 0

        lax.fori_loop(0, D // 128, turn_rows, 0, unroll=3)
        begin(steps[1])

    def weight_second():
        for at, load, matrix, source, target in (
            (0, loads[10], first_x, got_1x, send_2x),
            (1, loads[11], first_y, got_1y, send_2y),
        ):
            load.wait()
            arrived(steps[at])
            for start, width in lane_chunks(target.shape[1], 384):
                lanes = slice(start, start + width)
                target[:, lanes] = dot(matrix[...], source[:, lanes]).astype(BF16)
            begin(steps[2 + at])

    def weight_third():
        loads[12].wait()
        pad, count = second.shape[0] // n, send_z.shape[1]
        for at, source, base in ((2, got_2x, 0), (3, got_2y, split)):
            arrived(steps[at])
            for start, width in lane_chunks(source.shape[1], 384):
                total = dot(second[...], source[:, start : start + width]).astype(BF16)
                for i in range(n):
                    send_z[i, :, base + start : base + start + width] = total[i * pad : i * pad + count, :]
        begin(steps[4])

    half = got_h.shape[1]
    step_h = D - half

    def half_of(ref, which):
        return ref.at[:, pl.ds(pl.multiple_of(which * step_h, 128), half)]

    side_copy = remote(half_of(send_h, 1 - side), got_h, pair_send.at[2], pair_recv.at[2], (partner, seq))
    core_copy = remote(send_c, got_c, pair_send.at[3], pair_recv.at[3], (sibling, seq))

    def weight_fourth():
        arrived(steps[4])
        total = got_z[0].astype(F32)
        for i in range(1, n):
            total = total + got_z[i].astype(F32)
        send_h[...] = total.astype(BF16)
        side_copy.start()

    def weight_fifth():
        side_copy.wait_recv()
        near = send_h[:, pl.ds(pl.multiple_of(side * step_h, 128), half)].astype(F32)
        send_c[...] = (near + got_h[...].astype(F32)).astype(BF16)
        core_copy.start()

    def weight_last():
        core_copy.wait_recv()
        width = gws_o.shape[1]
        for i in range(4):

            @pl.when(dp == i)
            def _():
                base = i * width - (i // 2) * step_h
                near = send_c[...].astype(F32)[:, base : base + width]
                far = got_c[...].astype(F32)[:, base : base + width]
                gws_o[...] = far if i % 2 else near
                gwt_o[...] = near if i % 2 else far

    @pl.when(core == 0)
    def _():
        weight_product()

    cot_own.wait()
    rest = pl.ds(0, devices - 1)
    local(cot_got.at[rest], cot_got.at[rest], cot_recv.at[0]).wait()
    slabs_to_cells(cot_got, wide)
    for t in range(D // 128):
        at = slice(t * 128, (t + 1) * 128)
        gated[1, :, at] = (gate_t[:, at] * wide[t]).astype(BF16)
    loads[8].wait()

    def time_window(i, first, heads, start, width):
        at = pl.ds(start, width)
        total = gradients(first, heads, start, width, qt, kt, vt, up, shares, grads)
        attended[1, :, at] = total[0].astype(BF16)
        tiles = width // 128
        for t in range(3):
            for j in range(tiles):
                parts[t * tiles + j] = total[1 + t][:, j * 128 : (j + 1) * 128]

        def narrow(f, _):
            for t in range(3):
                for j in range(tiles):
                    to = pl.ds(pl.multiple_of(start + j * 128, 128), 128)
                    sent[f, t, :, to] = parts[t * tiles + j, pl.ds(f, CELL, stride=devices), :].astype(BF16)
            return 0

        lax.fori_loop(0, devices, narrow, 0, unroll=8)

        def send(k, _):
            peer = (seq + k) % devices
            remote(
                sent.at[peer, :, :, at], got.at[seq, :, :, at], t_send.at[i], t_recv.at[i], seq_peer(peer)
            ).start()
            return 0

        lax.fori_loop(1, devices, send, 0)
        local(sent.at[seq, :, :, at], got.at[seq, :, :, at], own_sem.at[6 + i]).start()

    def time_step(i, _):
        @pl.when(i < D // 384)
        def _():
            project(gated.at[1], wt, up, pl.multiple_of(i * 384, 128), 384)

        for j in range(HEADS // whole):
            score_time(i * (HEADS // whole) + j, qt, kt, vt, up, shares, grads)
        start = pl.multiple_of(i * WIN, 128)
        time_window(i, start // HEAD_DIM, CHUNK_HEADS, start, WIN)
        return 0

    lax.fori_loop(0, whole, time_step, 0)
    time_window(whole, tail // HEAD_DIM, HEADS - tail // HEAD_DIM, tail, D - tail)

    @pl.when(core == 0)
    def _():
        for copy in pair_copies(1):
            copy.start()
        weight_second()

    @pl.when(core == 1)
    def _():
        weight_product()
        weight_second()

    weight_third()
    weight_fourth()
    weight_fifth()

    windows = lane_chunks(D, WIN)
    for i, (start, width) in enumerate(windows):
        at = slice(start, start + width)
        local(sent.at[seq, :, :, at], got.at[seq, :, :, at], own_sem.at[6 + i]).wait()
        piece = got.at[rest, :, :, at]
        local(piece, piece, t_recv.at[i]).wait()

        def join(k, _):
            for t in range(3):
                slabs = [got[k * (16 // CELL) + j, t, :, at].astype(F32) for j in range(16 // CELL)]
                to = pl.ds(pl.multiple_of(k * 16, 16), 16)
                temporal[t, to, at] = jnp.concatenate(slabs, axis=0).astype(BF16)
            return 0

        lax.fori_loop(0, tokens // 16, join, 0, unroll=2)
    final = [local(temporal.at[i], out, store_sem.at[3 + i]) for i, out in enumerate((dqt_o, dkt_o, dvt_o))]
    for store in final:
        store.start()

    weight_last()
    for store in stores + final:
        store.wait()
    local(cot_slabs.at[rest], cot_slabs.at[rest], cot_send.at[0]).wait()
    for i, (start, width) in enumerate(windows):
        piece = sent.at[rest, :, :, start : start + width]
        local(piece, piece, t_send.at[i]).wait()
    for _, copies in steps:
        for copy in copies:
            copy.wait_send()
    for copy in pair_copies(0) + [side_copy, core_copy]:
        copy.wait_send()


def per_device(n, maps, qs, ks, vs, qt, kt, vt, cot, gate_s, gate_t, ws, wt):
    tokens = cot.shape[2]
    frames = qt.shape[1]
    devices = n * n * n
    rows_z = D // devices
    pad_y = padded(D // n // n)
    split = 640
    half = D // 2 + 64
    shape = cot.shape
    flat = lambda a: a.reshape(tokens, D)
    cells = lambda a: a.reshape(frames, CELL, D)
    any_space = pl.BlockSpec(memory_space=pl.ANY)
    vmem = pl.BlockSpec(memory_space=pltpu.VMEM)
    token = pltpu.VMEM((tokens, D), BF16)
    tokens_of = lambda k: pltpu.VMEM((k, tokens, D), BF16)
    raw = pltpu.VMEM((frames, CELL, D), BF16)
    weight = pltpu.VMEM((D, D), BF16)
    dma = lambda k: pltpu.SemaphoreType.DMA((k,))
    array = lambda *dims: pltpu.VMEM(dims, BF16)
    total = 4 * devices * tokens
    windows = len(lane_chunks(D, WIN))
    result = pl.pallas_call(
        functools.partial(kernel, n, total),
        out_shape=[jax.ShapeDtypeStruct((tokens, D), BF16)] * 6
        + [jax.ShapeDtypeStruct((rows_z, D // 4), F32)] * 2,
        in_specs=[any_space] * 13 + [vmem] * 2,
        out_specs=[any_space] * 6 + [vmem] * 2,
        scratch_shapes=[token] * 3
        + [raw] * 3
        + [token]
        + [weight] * 2
        + [pltpu.VMEM(m.shape, BF16) for m in maps]
        + [pltpu.VMEM((D // 128, tokens, 128), F32), pltpu.VMEM((3 * WIN // 128, tokens, 128), F32)]
        + [token] * 3
        + [raw] * 2
        + [tokens_of(2)] * 2
        + [token]
        + [array(HEADS, tokens, tokens)] * 2
        + [tokens_of(3)] * 2
        + [array(devices, 3, CELL, D)] * 2
        + [token] * 2
        + [weight, array(D, D - split), array(D, split), array(D, D - split)]
        + [array(n * pad_y, split), array(n * pad_y, D - split)] * 2
        + [array(n, rows_z, D)] * 2
        + [array(rows_z, D)]
        + [array(rows_z, half)] * 3
        + [dma(13), dma(6), dma(6 + windows)]
        + [dma(1)] * 2
        + [dma(windows)] * 2
        + [dma(5 * n)] * 2
        + [dma(4)] * 2,
        compiler_params=pltpu.CompilerParams(
            collective_id=0, has_side_effects=True, vmem_limit_bytes=60 * 1024 * 1024
        ),
    )(flat(qs), flat(ks), flat(vs), cells(qt), cells(kt), cells(vt), flat(cot), ws, wt, *maps, gate_s, gate_t)
    return tuple(a.reshape(shape) for a in result[:6]) + tuple(result[6:])


def solution(mesh):
    n = round(mesh.shape["seq"] ** (1 / 3))
    maps = row_maps(n)
    frames = P("dp", "seq", None, None)
    cells = P("dp", None, "seq", None)

    def run(*args):
        return per_device(n, [jnp.asarray(m) for m in maps], *args)

    return jax.shard_map(
        run,
        mesh=mesh,
        in_specs=(frames,) * 3 + (cells,) * 3 + (frames, P("dp", None), P("dp", None), P(), P()),
        out_specs=(frames,) * 6 + (P("seq", "dp"),) * 2,
        check_vma=False,
    )
```

time: 688 us -> 96.4 us (0.14); the launches traced: 679 us -> 96.2 us
  blocking collectives: 390 us -> 0 us
  Pallas kernels: 0 us -> 87 us
  waiting for transfers between devices: 70.2 us -> 0 us
  matrix products: 67.8 us -> 0 us
  local copies, waits for them, and re-layouts: 71.9 us -> 8.55 us
  starting transfers between devices: 53.9 us -> 0 us
  between operations: 15.2 us -> 0.68 us
  other arithmetic: 9.88 us -> 0 us
    unnamed x1 -> x0, blocking collectives: 390 us -> none
    pallas_call x0 -> x1, Pallas kernels: none -> 87 us  [per_device(): pl.pallas_call(functools.partial(kernel, n, total), out_shape=[jax.ShapeD...]
    unnamed x2 -> x0, waiting for transfers between devices: 70.2 us -> none
    dot_general x14 -> x0, matrix products: 58.3 us -> none  [the longest x2 14.3 us: attention_backward(): jnp.einsum('bchlm,bmche->blche', score_grad, keyset, preferred_element_ty...]
    all_to_all x5 -> x0, starting transfers between devices: 53.9 us -> none  [the longest x1 12.7 us: per_device(): lax.all_to_all(upstream_time, 'seq', split_axis=2, concat_axis=1, tiled=T...]
    reshape x10 -> x0, local copies, waits for them, and re-layouts: 18.8 us -> none  [the longest x8 16.4 us: per_device(): flat = tuple((item.reshape(cell_shape) for item in temporal))]
    mul x1 -> x0, local copies, waits for them, and re-layouts: 16 us -> none  [per_device(): jnp.stack([part_space, part_time], axis=1) * factor]
    another operation x4 -> x0, local copies, waits for them, and re-layouts: 10.6 us -> none
  transfers between devices with their start and end apart: 6 -> 0, of which waited for: 1 -> 0; matrix products, arithmetic and copies ran while one was open for 20% -> 0% of each run, Pallas kernels for 0% -> 0%
where the time goes in v2:
time: 96.4 us; the launch traced here: 96.2 us
  Pallas kernels  87 us (90%)
  local copies, waits for them, and re-layouts  8.55 us (9%)
    pallas_call x1, Pallas kernels, per_device(): pl.pallas_call(functools.partial(kernel, n, total), out_shape=[jax.ShapeD...  87 us
    unnamed x20, local copies, waits for them, and re-layouts  8.55 us

profile of v2, /device:TPU:1, one launch (start us, length us, event | category | flops | bytes accessed | tf_op | source)
XLA Modules:
  0.0 96.2 jit_solution(16308973226143715578)
XLA Ops:
  0.6 87.0 %shard_map.206 = (bf16[256,1152]{1,0:T(8,128)(2,1)}, bf16[256,1152]{1,0:T(8,128)(2,1)}, bf16[256,1152]{1,0:T(8,128)(2,1)}, bf16[256,1152]{1,0:T(8,128)(2,1)}, bf...) custom-call(bf16[256,1152]{1,0:T(8,128)(2,1)} %bitcast.13, ...), custom_call_target="tpu_custom_call" | custom-call | tf_op jit(solution)/shard_map/pallas_call | solution.py:628
  87.6 0.0 copy-start.3
  87.6 0.0 copy-start.2
  87.6 0.0 copy-start.1
  87.6 2.0 %copy.31 = bf16[1,1,256,1152]{3,2,1,0:T(8,128)(2,1)} copy(bf16[1,1,256,1152]{3,2,1,0:T(8,128)(2,1)} %bitcast.25) | data formatting | bytes 1179648
  89.7 0.0 copy-start
  89.7 2.0 %copy.32 = bf16[1,1,256,1152]{3,2,1,0:T(8,128)(2,1)} copy(bf16[1,1,256,1152]{3,2,1,0:T(8,128)(2,1)} %bitcast.24) | data formatting | bytes 1179648
  91.7 0.0 copy-done.3
  91.7 0.0 copy-start.5
  91.7 0.0 copy-start.4
  91.7 0.8 copy.33
  92.5 0.0 copy-done.2
  92.5 0.8 copy.34
  93.3 0.0 copy-done.1
  93.3 0.8 copy.35
  94.1 0.0 copy-done
  94.1 0.8 copy.36
  95.0 0.0 copy-done.5
  95.0 0.6 copy.37
  95.6 0.0 copy-done.4
  95.6 0.6 copy.38
Async XLA Ops:
  87.6 4.1 %copy-start.3 = (bf16[256,1152]{1,0:T(8,128)(2,1)S(1)}, bf16[256,1152]{1,0:T(8,128)(2,1)}, u32[]{:S(2)}) copy-start(bf16[256,1152]{1,0:T(8,128)(2,1)} %get-tuple-element.18) | copy-start | bytes 1769476
  87.6 4.9 %copy-start.2 = (bf16[256,1152]{1,0:T(8,128)(2,1)S(1)}, bf16[256,1152]{1,0:T(8,128)(2,1)}, u32[]{:S(2)}) copy-start(bf16[256,1152]{1,0:T(8,128)(2,1)} %get-tuple-element.19) | copy-start | bytes 1769476
  87.6 5.7 %copy-start.1 = (bf16[256,1152]{1,0:T(8,128)(2,1)S(1)}, bf16[256,1152]{1,0:T(8,128)(2,1)}, u32[]{:S(2)}) copy-start(bf16[256,1152]{1,0:T(8,128)(2,1)} %get-tuple-element.20) | copy-start | bytes 1769476
  89.7 4.4 %copy-start = (bf16[256,1152]{1,0:T(8,128)(2,1)S(1)}, bf16[256,1152]{1,0:T(8,128)(2,1)}, u32[]{:S(2)}) copy-start(bf16[256,1152]{1,0:T(8,128)(2,1)} %get-tuple-element.21) | copy-start | bytes 1769476
  91.7 3.3 %copy-start.5 = (f32[18,288]{1,0:T(8,128)S(1)}, f32[18,288]{1,0:T(8,128)}, u32[]{:S(2)}) copy-start(f32[18,288]{1,0:T(8,128)} %get-tuple-element.38) | copy-start | bytes 62212
  91.7 3.9 %copy-start.4 = (f32[18,288]{1,0:T(8,128)S(1)}, f32[18,288]{1,0:T(8,128)}, u32[]{:S(2)}) copy-start(f32[18,288]{1,0:T(8,128)} %get-tuple-element.39) | copy-start | bytes 62212

commit v3 on v2

--- a/solution.py
+++ b/solution.py
@@ -126,21 +126,19 @@
     grads[head] = expand(grad)
 
 
-def gradients(first, heads, start, width, q, k, v, u, shares, grads):
-    factor = 1.0 / math.sqrt(HEAD_DIM)
+def gradients(first, heads, start, width, q, k, v, u, shares, grads, wanted=range(4)):
     at = pl.ds(start, width)
     totals = [None] * 4
     for i in range(heads):
         head = first + i
         mask = head_mask(head, start, width)
-        terms = (
-            dot_rows(shares[head], v[:, at] * mask),
-            dot_rows(grads[head], k[:, at] * mask),
-            dot(grads[head], q[:, at] * mask),
-            dot(shares[head], u[:, at] * mask),
-        )
-        totals = [term if total is None else total + term for total, term in zip(totals, terms)]
-    return totals[0], totals[1] * factor, totals[2] * factor, totals[3]
+        for j in wanted:
+            matrix = grads if j in (1, 2) else shares
+            other = (v, k, q, u)[j]
+            term = (dot_rows if j < 2 else dot)(matrix[head], other[:, at] * mask)
+            totals[j] = term if totals[j] is None else totals[j] + term
+    factor = 1.0 / math.sqrt(HEAD_DIM)
+    return [totals[j] * factor if j in (1, 2) else totals[j] for j in wanted]
 
 
 def to_slabs(source, target, count):
@@ -232,10 +230,6 @@
     got_2y,
     send_z,
     got_z,
-    send_h,
-    got_h,
-    send_c,
-    got_c,
     load_sem,
     store_sem,
     own_sem,
@@ -245,6 +239,8 @@
     t_recv,
     w_send,
     w_recv,
+    z_send,
+    z_recv,
     pair_send,
     pair_recv,
 ):
@@ -253,11 +249,11 @@
     devices = n * n * n
     group, y = seq // n, seq % n
     x, z = group // n, group % n
-    core, side = dp % 2, dp // 2
+    side, core = dp // 2, dp % 2
     sibling = dp + 1 - 2 * core
-    partner = (dp + 2) % 4
     tokens = devices * CELL
-    split = product.shape[1] - got_1y.shape[1]
+    split, half = got_1x.shape[2], product.shape[2]
+    half_step = D - half
 
     loads = [
         pltpu.make_async_copy(source, target, load_sem.at[i])
@@ -291,8 +287,8 @@
     def x_peer(xx):
         return (dp, (xx * n + z) * n + y)
 
-    def z_peer(zz):
-        return (dp, (x * n + zz) * n + y)
+    def column_peer(q):
+        return (q // n, (x * n + q % n) * n + y)
 
     barrier = pltpu.get_barrier_semaphore()
 
@@ -304,11 +300,12 @@
         return 0
 
     lax.fori_loop(1, devices, greet_seq, 0)
-    greet((sibling, seq))
-    greet((partner, seq))
+    for i in range(1, 4):
+        for zz in range(n):
+            greet(column_peer((dp + i) % 4 * n + zz))
     loads[0].wait()
     to_slabs(cot, cot_slabs, devices)
-    pl.semaphore_wait(barrier, devices - 1 + 2)
+    pl.semaphore_wait(barrier, devices - 1 + 3 * n)
 
     def remote(source, target, send, recv, device):
         return pltpu.make_async_remote_copy(
@@ -333,6 +330,15 @@
     cot_own.start()
 
     gated[0] = (gate_s[...] * cot[...].astype(F32)).astype(BF16)
+
+    def pair_gated(kind):
+        k = 2 * kind
+        lanes = pl.ds(pl.multiple_of((1 - core) * half_step, 128), half)
+        return remote(
+            gated.at[kind, :, lanes], far_g.at[kind], pair_send.at[k], pair_recv.at[k], (sibling, seq)
+        )
+
+    pair_gated(0).start()
     loads[1].wait()
     for start, width in lane_chunks(D, 384):
         project(gated.at[0], ws, up, start, width)
@@ -357,16 +363,13 @@
     lax.fori_loop(0, whole, space_step, 0)
     space_window(tail // HEAD_DIM, HEADS - tail // HEAD_DIM, tail, D - tail)
 
-    def pair_copies(kind):
-        return [
-            remote(source.at[kind], target, pair_send.at[i], pair_recv.at[i], (sibling, seq))
-            for i, (source, target) in enumerate(((attended, far_a), (gated, far_g)))
-        ]
-
-    @pl.when(core == 1)
-    def _():
-        for copy in pair_copies(0):
-            copy.start()
+    def pair_attended(kind, i, at):
+        k = 2 * kind + i
+        return remote(
+            attended.at[kind, :, at], far_a.at[kind, :, at], pair_send.at[k], pair_recv.at[k], (sibling, seq)
+        )
+
+    pair_attended(0, 1, slice(0, D)).start()
 
     stores = [local(spatial.at[i], out, store_sem.at[i]) for i, out in enumerate((dqs_o, dks_o, dvs_o))]
     for store in stores:
@@ -381,24 +384,96 @@
     def rows(ref, at, count):
         return ref.at[pl.ds(pl.multiple_of(at * count, 16 if count % 16 == 0 else 8), count)]
 
-    def exchange(me, device, source, target, slot):
+    def exchange(me, device, source, target, slot, size=n):
         copies = []
-        for i in range(1, n):
-            peer = (me + i) % n
+        for i in range(1, size):
+            peer = (me + i) % size
             k = slot * n + i
             copies.append(remote(source(peer), target(me), w_send.at[k], w_recv.at[k], device(peer)))
         own = local(source(me), target(me), own_sem.at[1 + slot])
         return own, copies
 
-    count_1, count_2 = D // n, send_2x.shape[0] // n
+    count_1, count_2 = D // n, send_2x.shape[1] // n
     lanes_1 = slice(0, split)
-    steps = (
-        exchange(x, x_peer, lambda p: rows(product, p, count_1).at[:, lanes_1], lambda p: rows(got_1x, p, count_1), 0),
-        exchange(y, y_peer, lambda p: rows(turned, p, count_1), lambda p: rows(got_1y, p, count_1), 1),
-        exchange(y, y_peer, lambda p: rows(send_2x, p, count_2), lambda p: rows(got_2x, p, count_2), 2),
-        exchange(x, x_peer, lambda p: rows(send_2y, p, count_2), lambda p: rows(got_2y, p, count_2), 3),
-        exchange(z, z_peer, lambda p: send_z.at[p], lambda p: got_z.at[p], 4),
-    )
+
+    def all_steps(kind):
+        k = 4 * kind
+        return (
+            exchange(
+                x,
+                x_peer,
+                lambda p: rows(product.at[kind], p, count_1).at[:, lanes_1],
+                lambda p: rows(got_1x.at[kind], p, count_1),
+                k,
+            ),
+            exchange(
+                y,
+                y_peer,
+                lambda p: rows(turned.at[kind], p, count_1),
+                lambda p: rows(got_1y.at[kind], p, count_1),
+                k + 1,
+            ),
+            exchange(
+                y,
+                y_peer,
+                lambda p: rows(send_2x.at[kind], p, count_2),
+                lambda p: rows(got_2x.at[kind], p, count_2),
+                k + 2,
+            ),
+            exchange(
+                x,
+                x_peer,
+                lambda p: rows(send_2y.at[kind], p, count_2),
+                lambda p: rows(got_2y.at[kind], p, count_2),
+                k + 3,
+            ),
+        )
+
+    steps = (all_steps(0), all_steps(1))
+
+    owners = 2 * n
+    to_self = core == side
+
+    def owner_part(kind, e):
+        return send_z.at[kind, e % n, :, pl.ds(pl.multiple_of(e // n * 256, 128), 384)]
+
+    def owner_copy(kind, e):
+        place = side * n + z
+        return remote(
+            owner_part(kind, e),
+            got_z.at[kind, place],
+            z_send.at[kind * owners + e],
+            z_recv.at[kind * owners + place],
+            column_peer((2 * core + e // n) * n + e % n),
+        )
+
+    def owner_own(kind):
+        return local(owner_part(kind, core * n + z), got_z.at[kind, side * n + z], own_sem.at[9 + kind])
+
+    def owner_each(first, use_own, use):
+        @pl.when(to_self)
+        def _():
+            use_own()
+
+        @pl.when(jnp.logical_not(to_self))
+        def _():
+            use(first)
+
+        for i in range(1, owners):
+            use((first + i) % owners)
+
+    def begin_z(kind):
+        owner_each(core * n + z, lambda: owner_own(kind).start(), lambda e: owner_copy(kind, e).start())
+
+    def sent_z(kind):
+        owner_each(core * n + z, lambda: None, lambda e: owner_copy(kind, e).wait_send())
+
+    def arrived_z(kind):
+        def wait(s):
+            place = got_z.at[kind, s]
+            local(place, place, z_recv.at[kind * owners + s]).wait()
+
+        owner_each(side * n + z, lambda: owner_own(kind).wait(), wait)
 
     def begin(step):
         own, copies = step
@@ -414,96 +489,60 @@
 
     scale = 1.0 / math.sqrt(tokens_total)
 
-    def weight_product():
-        for copy in pair_copies(0):
-            copy.wait_recv()
-
-        def multiply(start, width):
-            to = slice(start, start + width)
-
-            def step(i, _):
-                at = pl.ds(pl.multiple_of(i * 128, 128), 128)
-                total = dot_rows(attended[core, :, at], gated[core, :, to]) + dot_rows(far_a[:, at], far_g[:, to])
-                product[at, to] = (total * scale).astype(BF16)
-                return 0
-
-            lax.fori_loop(0, D // 128, step, 0, unroll=3)
-
-        multiply(0, split)
-        begin(steps[0])
-        multiply(split, D - split)
-        loads[9].wait()
-
+    def product_rows(kind, first, blocks):
+        def step(i, _):
+            at = pl.ds(pl.multiple_of((first + i) * 128, 128), 128)
+            for start, width in lane_chunks(half, 384):
+                to = slice(start, start + width)
+                near = gated[kind, :, pl.ds(pl.multiple_of(core * half_step + start, 128), width)]
+                total = dot_rows(attended[kind, :, at], near) + dot_rows(far_a[kind, :, at], far_g[kind, :, to])
+                product[kind, at, to] = (total * scale).astype(BF16)
+            return 0
+
+        lax.fori_loop(0, blocks, step, 0, unroll=math.gcd(blocks, 3) if blocks > 2 else blocks)
+
+    def turn_product(kind):
         def turn_rows(i, _):
             at = pl.ds(pl.multiple_of(i * 128, 128), 128)
-            turned[at, :] = dot(turn[at, :], product[:, split:]).astype(BF16)
+            turned[kind, at, :] = dot(turn[at, :], product[kind, :, split:]).astype(BF16)
             return 0
 
         lax.fori_loop(0, D // 128, turn_rows, 0, unroll=3)
-        begin(steps[1])
-
-    def weight_second():
-        for at, load, matrix, source, target in (
-            (0, loads[10], first_x, got_1x, send_2x),
-            (1, loads[11], first_y, got_1y, send_2y),
-        ):
-            load.wait()
-            arrived(steps[at])
-            for start, width in lane_chunks(target.shape[1], 384):
-                lanes = slice(start, start + width)
-                target[:, lanes] = dot(matrix[...], source[:, lanes]).astype(BF16)
-            begin(steps[2 + at])
-
-    def weight_third():
-        loads[12].wait()
-        pad, count = second.shape[0] // n, send_z.shape[1]
+        begin(steps[kind][1])
+
+    def weight_second(kind):
+        for at, matrix, source, target in ((0, first_x, got_1x, send_2x), (1, first_y, got_1y, send_2y)):
+            arrived(steps[kind][at])
+            target[kind] = dot(matrix[...], source[kind]).astype(BF16)
+            begin(steps[kind][2 + at])
+
+    def weight_third(kind):
+        pad, count = second.shape[0] // n, send_z.shape[2]
         for at, source, base in ((2, got_2x, 0), (3, got_2y, split)):
-            arrived(steps[at])
-            for start, width in lane_chunks(source.shape[1], 384):
-                total = dot(second[...], source[:, start : start + width]).astype(BF16)
-                for i in range(n):
-                    send_z[i, :, base + start : base + start + width] = total[i * pad : i * pad + count, :]
-        begin(steps[4])
-
-    half = got_h.shape[1]
-    step_h = D - half
-
-    def half_of(ref, which):
-        return ref.at[:, pl.ds(pl.multiple_of(which * step_h, 128), half)]
-
-    side_copy = remote(half_of(send_h, 1 - side), got_h, pair_send.at[2], pair_recv.at[2], (partner, seq))
-    core_copy = remote(send_c, got_c, pair_send.at[3], pair_recv.at[3], (sibling, seq))
-
-    def weight_fourth():
-        arrived(steps[4])
-        total = got_z[0].astype(F32)
-        for i in range(1, n):
-            total = total + got_z[i].astype(F32)
-        send_h[...] = total.astype(BF16)
-        side_copy.start()
-
-    def weight_fifth():
-        side_copy.wait_recv()
-        near = send_h[:, pl.ds(pl.multiple_of(side * step_h, 128), half)].astype(F32)
-        send_c[...] = (near + got_h[...].astype(F32)).astype(BF16)
-        core_copy.start()
-
-    def weight_last():
-        core_copy.wait_recv()
-        width = gws_o.shape[1]
+            arrived(steps[kind][at])
+            total = dot(second[...], source[kind]).astype(BF16)
+            for i in range(n):
+                send_z[kind, i, :, base : base + total.shape[1]] = total[i * pad : i * pad + count, :]
+        begin_z(kind)
+
+    def weight_last(kind, out):
+        arrived_z(kind)
+        total = functools.reduce(lambda a, b: a + b, (got_z[kind, s].astype(F32) for s in range(owners)))
+        width = out.shape[1]
         for i in range(4):
 
             @pl.when(dp == i)
             def _():
-                base = i * width - (i // 2) * step_h
-                near = send_c[...].astype(F32)[:, base : base + width]
-                far = got_c[...].astype(F32)[:, base : base + width]
-                gws_o[...] = far if i % 2 else near
-                gwt_o[...] = near if i % 2 else far
-
-    @pl.when(core == 0)
-    def _():
-        weight_product()
+                base = i * width - i // 2 * half_step - i % 2 * 256
+                out[...] = total[:, base : base + width]
+
+    pair_gated(0).wait_recv()
+    pair_attended(0, 1, slice(0, D)).wait_recv()
+    product_rows(0, 0, D // 128)
+    begin(steps[0][0])
+    for load in loads[9:]:
+        load.wait()
+    turn_product(0)
 
     cot_own.wait()
     rest = pl.ds(0, devices - 1)
@@ -512,16 +551,22 @@
     for t in range(D // 128):
         at = slice(t * 128, (t + 1) * 128)
         gated[1, :, at] = (gate_t[:, at] * wide[t]).astype(BF16)
+
+    pair_gated(1).start()
     loads[8].wait()
+
+    def time_attended(first, heads, start, width):
+        at = pl.ds(start, width)
+        (total,) = gradients(first, heads, start, width, qt, kt, vt, up, shares, grads, (0,))
+        attended[1, :, at] = total.astype(BF16)
 
     def time_window(i, first, heads, start, width):
         at = pl.ds(start, width)
-        total = gradients(first, heads, start, width, qt, kt, vt, up, shares, grads)
-        attended[1, :, at] = total[0].astype(BF16)
+        total = gradients(first, heads, start, width, qt, kt, vt, up, shares, grads, (1, 2, 3))
         tiles = width // 128
         for t in range(3):
             for j in range(tiles):
-                parts[t * tiles + j] = total[1 + t][:, j * 128 : (j + 1) * 128]
+                parts[t * tiles + j] = total[t][:, j * 128 : (j + 1) * 128]
 
         def narrow(f, _):
             for t in range(3):
@@ -540,41 +585,63 @@
             return 0
 
         lax.fori_loop(1, devices, send, 0)
-        local(sent.at[seq, :, :, at], got.at[seq, :, :, at], own_sem.at[6 + i]).start()
-
-    def time_step(i, _):
-        @pl.when(i < D // 384)
-        def _():
-            project(gated.at[1], wt, up, pl.multiple_of(i * 384, 128), 384)
-
-        for j in range(HEADS // whole):
-            score_time(i * (HEADS // whole) + j, qt, kt, vt, up, shares, grads)
+        local(sent.at[seq, :, :, at], got.at[seq, :, :, at], own_sem.at[11 + i]).start()
+
+    def time_scores(first, count):
+        def step(i, _):
+            score_time(first + i, qt, kt, vt, up, shares, grads)
+            return 0
+
+        lax.fori_loop(0, count, step, 0, unroll=4)
+
+    def place_of(i):
         start = pl.multiple_of(i * WIN, 128)
-        time_window(i, start // HEAD_DIM, CHUNK_HEADS, start, WIN)
+        return start // HEAD_DIM, CHUNK_HEADS, start, WIN
+
+    last = (tail // HEAD_DIM, HEADS - tail // HEAD_DIM, tail, D - tail)
+    early = (slice(0, WIN), slice(WIN, D))
+
+    project(gated.at[1], wt, up, 0, 384)
+    time_scores(0, 4)
+    time_attended(0, 4, 0, WIN)
+    pair_attended(1, 1, early[0]).start()
+    time_window(0, 0, 4, 0, WIN)
+
+    for start, width in lane_chunks(D, 384)[1:]:
+        project(gated.at[1], wt, up, start, width)
+    time_scores(4, HEADS - 4)
+
+    def attended_step(i, _):
+        time_attended(*place_of(i))
         return 0
 
-    lax.fori_loop(0, whole, time_step, 0)
-    time_window(whole, tail // HEAD_DIM, HEADS - tail // HEAD_DIM, tail, D - tail)
-
-    @pl.when(core == 0)
-    def _():
-        for copy in pair_copies(1):
-            copy.start()
-        weight_second()
-
-    @pl.when(core == 1)
-    def _():
-        weight_product()
-        weight_second()
-
-    weight_third()
-    weight_fourth()
-    weight_fifth()
+    lax.fori_loop(1, whole, attended_step, 0)
+    time_attended(*last)
+    pair_attended(1, 2, early[1]).start()
+    time_window(1, *place_of(1))
+    pair_gated(1).wait_recv()
+    for i, at in enumerate(early):
+        pair_attended(1, 1 + i, at).wait_recv()
+    product_rows(1, 0, D // 128)
+    begin(steps[1][0])
+    turn_product(1)
+    weight_second(0)
+
+    def window_step(i, _):
+        time_window(i, *place_of(i))
+        return 0
+
+    lax.fori_loop(2, whole, window_step, 0)
+    time_window(whole, *last)
+    weight_third(0)
+    weight_second(1)
+    weight_third(1)
+    weight_last(0, gws_o)
 
     windows = lane_chunks(D, WIN)
     for i, (start, width) in enumerate(windows):
         at = slice(start, start + width)
-        local(sent.at[seq, :, :, at], got.at[seq, :, :, at], own_sem.at[6 + i]).wait()
+        local(sent.at[seq, :, :, at], got.at[seq, :, :, at], own_sem.at[11 + i]).wait()
         piece = got.at[rest, :, :, at]
         local(piece, piece, t_recv.at[i]).wait()
 
@@ -590,18 +657,37 @@
     for store in final:
         store.start()
 
-    weight_last()
+    weight_last(1, gwt_o)
     for store in stores + final:
         store.wait()
     local(cot_slabs.at[rest], cot_slabs.at[rest], cot_send.at[0]).wait()
     for i, (start, width) in enumerate(windows):
         piece = sent.at[rest, :, :, start : start + width]
         local(piece, piece, t_send.at[i]).wait()
-    for _, copies in steps:
-        for copy in copies:
-            copy.wait_send()
-    for copy in pair_copies(0) + [side_copy, core_copy]:
-        copy.wait_send()
+    for kind in range(2):
+        for _, copies in steps[kind]:
+            for copy in copies:
+                copy.wait_send()
+        sent_z(kind)
+        pair_gated(kind).wait_send()
+    pair_attended(0, 1, slice(0, D)).wait_send()
+    for i, at in enumerate(early):
+        pair_attended(1, 1 + i, at).wait_send()
+
+
+def hand_over(*refs):
+    sources, targets, buffers, (in_sem, out_sem) = refs[:6], refs[6:12], refs[12:18], refs[18:]
+    steps = [
+        (pltpu.make_async_copy(s, b, in_sem.at[i]), pltpu.make_async_copy(b, t, out_sem.at[i]))
+        for i, (s, b, t) in enumerate(zip(sources, buffers, targets))
+    ]
+    for come, _ in steps:
+        come.start()
+    for come, go in steps:
+        come.wait()
+        go.start()
+    for _, go in steps:
+        go.wait()
 
 
 def per_device(n, maps, qs, ks, vs, qt, kt, vt, cot, gate_s, gate_t, ws, wt):
@@ -610,8 +696,7 @@
     devices = n * n * n
     rows_z = D // devices
     pad_y = padded(D // n // n)
-    split = 640
-    half = D // 2 + 64
+    split, half = 384, D // 2 + 64
     shape = cot.shape
     flat = lambda a: a.reshape(tokens, D)
     cells = lambda a: a.reshape(frames, CELL, D)
@@ -644,22 +729,28 @@
         + [array(HEADS, tokens, tokens)] * 2
         + [tokens_of(3)] * 2
         + [array(devices, 3, CELL, D)] * 2
-        + [token] * 2
-        + [weight, array(D, D - split), array(D, split), array(D, D - split)]
-        + [array(n * pad_y, split), array(n * pad_y, D - split)] * 2
-        + [array(n, rows_z, D)] * 2
-        + [array(rows_z, D)]
-        + [array(rows_z, half)] * 3
-        + [dma(13), dma(6), dma(6 + windows)]
+        + [tokens_of(2), array(2, tokens, half)]
+        + [array(2, D, half), array(2, D, half - split), array(2, D, split), array(2, D, half - split)]
+        + [array(2, n * pad_y, split), array(2, n * pad_y, half - split)] * 2
+        + [array(2, n, rows_z, half), array(2, 2 * n, rows_z, 384)]
+        + [dma(13), dma(6), dma(11 + windows)]
         + [dma(1)] * 2
         + [dma(windows)] * 2
-        + [dma(5 * n)] * 2
-        + [dma(4)] * 2,
+        + [dma(8 * n)] * 2
+        + [dma(4 * n)] * 2
+        + [dma(5)] * 2,
         compiler_params=pltpu.CompilerParams(
             collective_id=0, has_side_effects=True, vmem_limit_bytes=60 * 1024 * 1024
         ),
     )(flat(qs), flat(ks), flat(vs), cells(qt), cells(kt), cells(vt), flat(cot), ws, wt, *maps, gate_s, gate_t)
-    return tuple(a.reshape(shape) for a in result[:6]) + tuple(result[6:])
+    tensors = pl.pallas_call(
+        hand_over,
+        out_shape=[jax.ShapeDtypeStruct((tokens, D), BF16)] * 6,
+        in_specs=[any_space] * 6,
+        out_specs=[any_space] * 6,
+        scratch_shapes=[token] * 6 + [dma(6)] * 2,
+    )(*result[:6])
+    return tuple(a.reshape(shape) for a in tensors) + tuple(result[6:])
 
 
 def solution(mesh):

time: 96.4 us -> 87.5 us (0.908)
  local copies, waits for them, and re-layouts: 8.55 us -> 1.24 us
  Pallas kernels: 87 us -> 85.5 us
    unnamed x20 -> x6, local copies, waits for them, and re-layouts: 8.55 us -> 1.24 us
    pallas_call x1, Pallas kernels: 87 us -> 82.5 us  [per_device(): pl.pallas_call(functools.partial(kernel, n, total), out_shape=[jax.ShapeD...]
    pallas_call x0 -> x1, Pallas kernels: none -> 2.97 us  [per_device(): pl.pallas_call(hand_over, out_shape=[jax.ShapeDtypeStruct((tokens, D), BF...]
where the time goes in v3:
time: 87.5 us; the launch traced here: 87.4 us
  Pallas kernels  85.5 us (98%)
  local copies, waits for them, and re-layouts  1.24 us (1%)
    pallas_call x1, Pallas kernels, per_device(): pl.pallas_call(functools.partial(kernel, n, total), out_shape=[jax.ShapeD...  82.5 us
    pallas_call x1, Pallas kernels, per_device(): pl.pallas_call(hand_over, out_shape=[jax.ShapeDtypeStruct((tokens, D), BF...  2.97 us

profile of v3, /device:TPU:1, one launch (start us, length us, event | category | flops | bytes accessed | tf_op | source)
XLA Modules:
  0.0 87.4 jit_solution(10238849216786027430)
XLA Ops:
  0.6 82.5 %shard_map.206 = (bf16[256,1152]{1,0:T(8,128)(2,1)}, bf16[256,1152]{1,0:T(8,128)(2,1)}, bf16[256,1152]{1,0:T(8,128)(2,1)}, bf16[256,1152]{1,0:T(8,128)(2,1)}, bf...) custom-call(bf16[256,1152]{1,0:T(8,128)(2,1)} %bitcast.13, ...), custom_call_target="tpu_custom_call" | custom-call | tf_op jit(solution)/shard_map/pallas_call | solution.py:713
  83.1 0.0 copy-start.1
  83.1 0.0 copy-start
  83.2 3.0 %shard_map.207 = (bf16[256,1152]{1,0:T(8,128)(2,1)}, bf16[256,1152]{1,0:T(8,128)(2,1)}, bf16[256,1152]{1,0:T(8,128)(2,1)}, bf16[256,1152]{1,0:T(8,128)(2,1)}, bf...) custom-call(bf16[256,1152]{1,0:T(8,128)(2,1)} %get-tuple-element.22.refs_0_, ...), custom_call_target="tpu_custom_call" | custom-call | tf_op jit(solution)/shard_map/pallas_call | solution.py:746
  86.1 0.0 copy-done.1
  86.1 0.6 copy.25
  86.8 0.0 copy-done
  86.8 0.6 copy.26
Async XLA Ops:
  83.1 3.0 %copy-start.1 = (f32[18,288]{1,0:T(8,128)S(1)}, f32[18,288]{1,0:T(8,128)}, u32[]{:S(2)}) copy-start(f32[18,288]{1,0:T(8,128)} %get-tuple-element.50) | copy-start | bytes 62212
  83.1 3.6 %copy-start = (f32[18,288]{1,0:T(8,128)S(1)}, f32[18,288]{1,0:T(8,128)}, u32[]{:S(2)}) copy-start(f32[18,288]{1,0:T(8,128)} %get-tuple-element.51) | copy-start | bytes 62212

commit v4 on v3

--- a/solution.py
+++ b/solution.py
@@ -14,6 +14,7 @@
 D = HEADS * HEAD_DIM
 CELL = 4
 WIN = 256
+FIRST = 128
 MESH = pl.DeviceIdType.MESH
 F32 = jnp.float32
 BF16 = jnp.bfloat16
@@ -216,6 +217,8 @@
     grads,
     spatial,
     temporal,
+    sent_0,
+    got_0,
     sent,
     got,
     far_a,
@@ -341,27 +344,33 @@
     pair_gated(0).start()
     loads[1].wait()
     for start, width in lane_chunks(D, 384):
-        project(gated.at[0], ws, up, start, width)
+        project(gated.at[0], ws, up.at[0], start, width)
     for load in loads[2:5]:
         load.wait()
-    scores_space(qs, ks, vs, up, shares, grads)
+    space = (qs, ks, vs, up.at[0], shares.at[0], grads.at[0])
+    scores_space(*space)
     whole = D // WIN
     tail = whole * WIN
 
+    def space_attended(first, heads, start, width):
+        (total,) = gradients(first, heads, start, width, *space, (0,))
+        attended[0, :, pl.ds(start, width)] = total.astype(BF16)
+
     def space_window(first, heads, start, width):
-        at = pl.ds(start, width)
-        total = gradients(first, heads, start, width, qs, ks, vs, up, shares, grads)
-        attended[0, :, at] = total[0].astype(BF16)
+        total = gradients(first, heads, start, width, *space, (1, 2, 3))
         for i in range(3):
-            spatial[i, :, at] = total[1 + i].astype(BF16)
-
-    def space_step(i, _):
-        start = pl.multiple_of(i * WIN, 128)
-        space_window(start // HEAD_DIM, CHUNK_HEADS, start, WIN)
-        return 0
-
-    lax.fori_loop(0, whole, space_step, 0)
-    space_window(tail // HEAD_DIM, HEADS - tail // HEAD_DIM, tail, D - tail)
+            spatial[i, :, pl.ds(start, width)] = total[i].astype(BF16)
+
+    def space_windows(window_of):
+        def step(i, _):
+            start = pl.multiple_of(i * WIN, 128)
+            window_of(start // HEAD_DIM, CHUNK_HEADS, start, WIN)
+            return 0
+
+        lax.fori_loop(0, whole, step, 0)
+        window_of(tail // HEAD_DIM, HEADS - tail // HEAD_DIM, tail, D - tail)
+
+    space_windows(space_attended)
 
     def pair_attended(kind, i, at):
         k = 2 * kind + i
@@ -370,10 +379,6 @@
         )
 
     pair_attended(0, 1, slice(0, D)).start()
-
-    stores = [local(spatial.at[i], out, store_sem.at[i]) for i, out in enumerate((dqs_o, dks_o, dvs_o))]
-    for store in stores:
-        store.start()
 
     for raw, target, load in ((qraw, qt, loads[5]), (kraw, kt, loads[6]), (vraw, vt, loads[7])):
         load.wait()
@@ -435,7 +440,7 @@
     to_self = core == side
 
     def owner_part(kind, e):
-        return send_z.at[kind, e % n, :, pl.ds(pl.multiple_of(e // n * 256, 128), 384)]
+        return send_z.at[kind, e % n, :, :, pl.ds(pl.multiple_of(e // n * 256, 128), 384)]
 
     def owner_copy(kind, e):
         place = side * n + z
@@ -522,12 +527,15 @@
             arrived(steps[kind][at])
             total = dot(second[...], source[kind]).astype(BF16)
             for i in range(n):
-                send_z[kind, i, :, base : base + total.shape[1]] = total[i * pad : i * pad + count, :]
+                for j in range(count):
+                    row = i * pad + 2 * j
+                    send_z[kind, i, j, :, base : base + total.shape[1]] = total[row : row + 2, :]
         begin_z(kind)
 
     def weight_last(kind, out):
         arrived_z(kind)
         total = functools.reduce(lambda a, b: a + b, (got_z[kind, s].astype(F32) for s in range(owners)))
+        total = jnp.concatenate([total[j] for j in range(total.shape[0])], axis=0)
         width = out.shape[1]
         for i in range(4):
 
@@ -555,15 +563,20 @@
     pair_gated(1).start()
     loads[8].wait()
 
+    time = (qt, kt, vt, up.at[1], shares.at[1], grads.at[1])
+
     def time_attended(first, heads, start, width):
         at = pl.ds(start, width)
-        (total,) = gradients(first, heads, start, width, qt, kt, vt, up, shares, grads, (0,))
+        (total,) = gradients(first, heads, start, width, *time, (0,))
         attended[1, :, at] = total.astype(BF16)
 
+    def pieces(i, width):
+        return (sent_0, got_0) if width == FIRST else (sent.at[i - 1], got.at[i - 1])
+
     def time_window(i, first, heads, start, width):
-        at = pl.ds(start, width)
-        total = gradients(first, heads, start, width, qt, kt, vt, up, shares, grads, (1, 2, 3))
+        total = gradients(first, heads, start, width, *time, (1, 2, 3))
         tiles = width // 128
+        out, come = pieces(i, width)
         for t in range(3):
             for j in range(tiles):
                 parts[t * tiles + j] = total[t][:, j * 128 : (j + 1) * 128]
@@ -571,54 +584,53 @@
         def narrow(f, _):
             for t in range(3):
                 for j in range(tiles):
-                    to = pl.ds(pl.multiple_of(start + j * 128, 128), 128)
-                    sent[f, t, :, to] = parts[t * tiles + j, pl.ds(f, CELL, stride=devices), :].astype(BF16)
+                    slab = parts[t * tiles + j, pl.ds(f, CELL, stride=devices), :]
+                    out[f, t, :, j * 128 : (j + 1) * 128] = slab.astype(BF16)
             return 0
 
         lax.fori_loop(0, devices, narrow, 0, unroll=8)
 
         def send(k, _):
             peer = (seq + k) % devices
-            remote(
-                sent.at[peer, :, :, at], got.at[seq, :, :, at], t_send.at[i], t_recv.at[i], seq_peer(peer)
-            ).start()
+            remote(out.at[peer], come.at[seq], t_send.at[i], t_recv.at[i], seq_peer(peer)).start()
             return 0
 
         lax.fori_loop(1, devices, send, 0)
-        local(sent.at[seq, :, :, at], got.at[seq, :, :, at], own_sem.at[11 + i]).start()
+        local(out.at[seq], come.at[seq], own_sem.at[11 + i]).start()
 
     def time_scores(first, count):
         def step(i, _):
-            score_time(first + i, qt, kt, vt, up, shares, grads)
+            score_time(first + i, *time)
             return 0
 
-        lax.fori_loop(0, count, step, 0, unroll=4)
+        lax.fori_loop(0, count, step, 0, unroll=count if count < 5 else count // 2)
 
     def place_of(i):
-        start = pl.multiple_of(i * WIN, 128)
-        return start // HEAD_DIM, CHUNK_HEADS, start, WIN
-
-    last = (tail // HEAD_DIM, HEADS - tail // HEAD_DIM, tail, D - tail)
-    early = (slice(0, WIN), slice(WIN, D))
-
-    project(gated.at[1], wt, up, 0, 384)
-    time_scores(0, 4)
-    time_attended(0, 4, 0, WIN)
+        start = pl.multiple_of((i - 1) * WIN + FIRST, 128)
+        return jnp.minimum(start // HEAD_DIM, HEADS - CHUNK_HEADS), CHUNK_HEADS, start, WIN
+
+    opening = (0, -(-FIRST // HEAD_DIM), 0, FIRST)
+    early = (slice(0, FIRST), slice(FIRST, D))
+
+    project(gated.at[1], wt, up.at[1], 0, 256)
+    time_scores(0, opening[1])
+    time_window(0, *opening)
+
+    project(gated.at[1], wt, up.at[1], 256, 512)
+    time_scores(opening[1], CHUNK_HEADS + 1 - opening[1])
+    time_window(1, *place_of(1))
+
+    project(gated.at[1], wt, up.at[1], 768, 384)
+    time_scores(CHUNK_HEADS + 1, HEADS - CHUNK_HEADS - 1)
+    time_attended(*opening)
     pair_attended(1, 1, early[0]).start()
-    time_window(0, 0, 4, 0, WIN)
-
-    for start, width in lane_chunks(D, 384)[1:]:
-        project(gated.at[1], wt, up, start, width)
-    time_scores(4, HEADS - 4)
 
     def attended_step(i, _):
         time_attended(*place_of(i))
         return 0
 
-    lax.fori_loop(1, whole, attended_step, 0)
-    time_attended(*last)
+    lax.fori_loop(1, whole + 1, attended_step, 0)
     pair_attended(1, 2, early[1]).start()
-    time_window(1, *place_of(1))
     pair_gated(1).wait_recv()
     for i, at in enumerate(early):
         pair_attended(1, 1 + i, at).wait_recv()
@@ -631,39 +643,45 @@
         time_window(i, *place_of(i))
         return 0
 
-    lax.fori_loop(2, whole, window_step, 0)
-    time_window(whole, *last)
+    lax.fori_loop(2, whole + 1, window_step, 0)
+    space_windows(space_window)
+    space_stores = [local(spatial.at[i], out, store_sem.at[i]) for i, out in enumerate((dqs_o, dks_o, dvs_o))]
+    for store in space_stores:
+        store.start()
     weight_third(0)
     weight_second(1)
     weight_third(1)
     weight_last(0, gws_o)
 
-    windows = lane_chunks(D, WIN)
-    for i, (start, width) in enumerate(windows):
+    outs = (dqt_o, dkt_o, dvt_o)
+    stores = [(temporal.at[i], out) for i, out in enumerate(outs)]
+    final = []
+    for i in range(whole + 1):
+        start, width = (0, FIRST) if i == 0 else ((i - 1) * WIN + FIRST, WIN)
         at = slice(start, start + width)
-        local(sent.at[seq, :, :, at], got.at[seq, :, :, at], own_sem.at[11 + i]).wait()
-        piece = got.at[rest, :, :, at]
-        local(piece, piece, t_recv.at[i]).wait()
+        out, come = pieces(i, width)
+        local(out.at[seq], come.at[seq], own_sem.at[11 + i]).wait()
+        local(come.at[rest], come.at[rest], t_recv.at[i]).wait()
 
         def join(k, _):
             for t in range(3):
-                slabs = [got[k * (16 // CELL) + j, t, :, at].astype(F32) for j in range(16 // CELL)]
+                slabs = [come[k * (16 // CELL) + j, t].astype(F32) for j in range(16 // CELL)]
                 to = pl.ds(pl.multiple_of(k * 16, 16), 16)
                 temporal[t, to, at] = jnp.concatenate(slabs, axis=0).astype(BF16)
             return 0
 
         lax.fori_loop(0, tokens // 16, join, 0, unroll=2)
-    final = [local(temporal.at[i], out, store_sem.at[3 + i]) for i, out in enumerate((dqt_o, dkt_o, dvt_o))]
-    for store in final:
-        store.start()
+        for t, (source, target) in enumerate(stores):
+            final.append(local(source.at[:, at], target.at[:, at], store_sem.at[3 + 3 * i + t]))
+            final[-1].start()
 
     weight_last(1, gwt_o)
-    for store in stores + final:
+    for store in space_stores + final:
         store.wait()
     local(cot_slabs.at[rest], cot_slabs.at[rest], cot_send.at[0]).wait()
-    for i, (start, width) in enumerate(windows):
-        piece = sent.at[rest, :, :, start : start + width]
-        local(piece, piece, t_send.at[i]).wait()
+    for i in range(whole + 1):
+        out, _ = pieces(i, FIRST if i == 0 else WIN)
+        local(out.at[rest], out.at[rest], t_send.at[i]).wait()
     for kind in range(2):
         for _, copies in steps[kind]:
             for copy in copies:
@@ -709,7 +727,7 @@
     dma = lambda k: pltpu.SemaphoreType.DMA((k,))
     array = lambda *dims: pltpu.VMEM(dims, BF16)
     total = 4 * devices * tokens
-    windows = len(lane_chunks(D, WIN))
+    windows = 1 + (D - FIRST) // WIN
     result = pl.pallas_call(
         functools.partial(kernel, n, total),
         out_shape=[jax.ShapeDtypeStruct((tokens, D), BF16)] * 6
@@ -725,15 +743,16 @@
         + [token] * 3
         + [raw] * 2
         + [tokens_of(2)] * 2
-        + [token]
-        + [array(HEADS, tokens, tokens)] * 2
+        + [tokens_of(2)]
+        + [array(2, HEADS, tokens, tokens)] * 2
         + [tokens_of(3)] * 2
-        + [array(devices, 3, CELL, D)] * 2
+        + [array(devices, 3, CELL, FIRST)] * 2
+        + [array(windows - 1, devices, 3, CELL, WIN)] * 2
         + [tokens_of(2), array(2, tokens, half)]
         + [array(2, D, half), array(2, D, half - split), array(2, D, split), array(2, D, half - split)]
         + [array(2, n * pad_y, split), array(2, n * pad_y, half - split)] * 2
-        + [array(2, n, rows_z, half), array(2, 2 * n, rows_z, 384)]
-        + [dma(13), dma(6), dma(11 + windows)]
+        + [array(2, n, rows_z // 2, 2, half), array(2, 2 * n, rows_z // 2, 2, 384)]
+        + [dma(13), dma(3 + 3 * windows), dma(11 + windows)]
         + [dma(1)] * 2
         + [dma(windows)] * 2
         + [dma(8 * n)] * 2

time: 87.5 us -> 84.5 us (0.966)
  Pallas kernels: 85.5 us -> 82.4 us
    pallas_call x1, Pallas kernels: 82.5 us -> 79.5 us  [per_device(): pl.pallas_call(functools.partial(kernel, n, total), out_shape=[jax.ShapeD...]
where the time goes in v4:
time: 84.5 us; the launch traced here: 84.4 us
  Pallas kernels  82.4 us (98%)
  local copies, waits for them, and re-layouts  1.24 us (1%)
    pallas_call x1, Pallas kernels, per_device(): pl.pallas_call(functools.partial(kernel, n, total), out_shape=[jax.ShapeD...  79.5 us
    pallas_call x1, Pallas kernels, per_device(): pl.pallas_call(hand_over, out_shape=[jax.ShapeDtypeStruct((tokens, D), BF...  2.97 us

profile of v4, /device:TPU:1, one launch (start us, length us, event | category | flops | bytes accessed | tf_op | source)
XLA Modules:
  0.0 84.4 jit_solution(2729682309766784749)
XLA Ops:
  0.6 79.5 %shard_map.206 = (bf16[256,1152]{1,0:T(8,128)(2,1)}, bf16[256,1152]{1,0:T(8,128)(2,1)}, bf16[256,1152]{1,0:T(8,128)(2,1)}, bf16[256,1152]{1,0:T(8,128)(2,1)}, bf...) custom-call(bf16[256,1152]{1,0:T(8,128)(2,1)} %bitcast.13, ...), custom_call_target="tpu_custom_call" | custom-call | tf_op jit(solution)/shard_map/pallas_call | solution.py:731
  80.1 0.0 copy-start.1
  80.1 0.0 copy-start
  80.1 3.0 %shard_map.207 = (bf16[256,1152]{1,0:T(8,128)(2,1)}, bf16[256,1152]{1,0:T(8,128)(2,1)}, bf16[256,1152]{1,0:T(8,128)(2,1)}, bf16[256,1152]{1,0:T(8,128)(2,1)}, bf...) custom-call(bf16[256,1152]{1,0:T(8,128)(2,1)} %get-tuple-element.22.refs_0_, ...), custom_call_target="tpu_custom_call" | custom-call | tf_op jit(solution)/shard_map/pallas_call | solution.py:765
  83.1 0.0 copy-done.1
  83.1 0.6 copy.25
  83.7 0.0 copy-done
  83.7 0.6 copy.26
Async XLA Ops:
  80.1 3.0 %copy-start.1 = (f32[18,288]{1,0:T(8,128)S(1)}, f32[18,288]{1,0:T(8,128)}, u32[]{:S(2)}) copy-start(f32[18,288]{1,0:T(8,128)} %get-tuple-element.50) | copy-start | bytes 62212
  80.1 3.6 %copy-start = (f32[18,288]{1,0:T(8,128)S(1)}, f32[18,288]{1,0:T(8,128)}, u32[]{:S(2)}) copy-start(f32[18,288]{1,0:T(8,128)} %get-tuple-element.51) | copy-start | bytes 62212

commit v5 on v4

--- a/solution.py
+++ b/solution.py
@@ -631,6 +631,7 @@
 
     lax.fori_loop(1, whole + 1, attended_step, 0)
     pair_attended(1, 2, early[1]).start()
+    time_window(2, *place_of(2))
     pair_gated(1).wait_recv()
     for i, at in enumerate(early):
         pair_attended(1, 1 + i, at).wait_recv()
@@ -643,13 +644,13 @@
         time_window(i, *place_of(i))
         return 0
 
-    lax.fori_loop(2, whole + 1, window_step, 0)
+    lax.fori_loop(3, whole + 1, window_step, 0)
+    weight_third(0)
+    weight_second(1)
     space_windows(space_window)
     space_stores = [local(spatial.at[i], out, store_sem.at[i]) for i, out in enumerate((dqs_o, dks_o, dvs_o))]
     for store in space_stores:
         store.start()
-    weight_third(0)
-    weight_second(1)
     weight_third(1)
     weight_last(0, gws_o)
 

time: 84.5 us -> 84.1 us (level)
  no operation moved by 1% of the time
where the time goes in v5:
time: 84.1 us; the launch traced here: 84 us
  Pallas kernels  82 us (98%)
  local copies, waits for them, and re-layouts  1.24 us (1%)
    pallas_call x1, Pallas kernels, per_device(): pl.pallas_call(functools.partial(kernel, n, total), out_shape=[jax.ShapeD...  79.1 us
    pallas_call x1, Pallas kernels, per_device(): pl.pallas_call(hand_over, out_shape=[jax.ShapeDtypeStruct((tokens, D), BF...  2.97 us

profile of v5, /device:TPU:1, one launch (start us, length us, event | category | flops | bytes accessed | tf_op | source)
XLA Modules:
  0.0 84.0 jit_solution(10581842993165412914)
XLA Ops:
  0.6 79.1 %shard_map.206 = (bf16[256,1152]{1,0:T(8,128)(2,1)}, bf16[256,1152]{1,0:T(8,128)(2,1)}, bf16[256,1152]{1,0:T(8,128)(2,1)}, bf16[256,1152]{1,0:T(8,128)(2,1)}, bf...) custom-call(bf16[256,1152]{1,0:T(8,128)(2,1)} %bitcast.13, ...), custom_call_target="tpu_custom_call" | custom-call | tf_op jit(solution)/shard_map/pallas_call | solution.py:732
  79.7 0.0 copy-start.1
  79.7 0.0 copy-start
  79.7 3.0 %shard_map.207 = (bf16[256,1152]{1,0:T(8,128)(2,1)}, bf16[256,1152]{1,0:T(8,128)(2,1)}, bf16[256,1152]{1,0:T(8,128)(2,1)}, bf16[256,1152]{1,0:T(8,128)(2,1)}, bf...) custom-call(bf16[256,1152]{1,0:T(8,128)(2,1)} %get-tuple-element.22.refs_0_, ...), custom_call_target="tpu_custom_call" | custom-call | tf_op jit(solution)/shard_map/pallas_call | solution.py:766
  82.7 0.0 copy-done.1
  82.7 0.6 copy.25
  83.3 0.0 copy-done
  83.3 0.6 copy.26
Async XLA Ops:
  79.7 3.0 %copy-start.1 = (f32[18,288]{1,0:T(8,128)S(1)}, f32[18,288]{1,0:T(8,128)}, u32[]{:S(2)}) copy-start(f32[18,288]{1,0:T(8,128)} %get-tuple-element.50) | copy-start | bytes 62212
  79.7 3.6 %copy-start = (f32[18,288]{1,0:T(8,128)S(1)}, f32[18,288]{1,0:T(8,128)}, u32[]{:S(2)}) copy-start(f32[18,288]{1,0:T(8,128)} %get-tuple-element.51) | copy-start | bytes 62212
